TPU v7x, 32 devices: a whole 2x2x4 slice. The times are simulated.
32 devices in a mesh: cx: 4 (over z), cy: 4 (over y, x), orb: 2 (over core).
Axes of the slice: x: 2, y: 2, z: 4, core: 2. Of those that a mesh axis runs over, the one named last changes fastest.
Arguments:
- coeffs: bfloat16 [16, 32, 128, 1024], P('cx', 'cy', None, 'orb'), may hold values from -6 to 6
- occupation: float32 [1024], P('orb'), may hold values from 0.05 to 2
- energies: float32 [1024], P('orb'), may hold values from -1.5 to 0.5
- row_atom: int32 [16, 32, 128], P('cx', 'cy', 'orb'), may hold values from 0 to 7, never falling along the last dimension, each value on 1 to 32 neighbouring positions
- pair_first: int32 [4, 4, 64], P('cx', 'cy'), may hold values from 0 to 31
- pair_second: int32 [4, 4, 64], P('cx', 'cy'), may hold values from 0 to 59, as said below
- pair_count: int32 [4, 4], P('cx', 'cy'), may hold values from 16 to 64, as said below
- deriv_h: bfloat16 [4, 4, 64, 3, 128, 128], P('cx', 'cy', None, None, 'orb'), may hold values from -0.0029296875 to 0.0029296875
- deriv_s: bfloat16 [4, 4, 64, 3, 128, 128], P('cx', 'cy', None, None, 'orb'), may hold values from -0.0029296875 to 0.0029296875
Outputs:
- forces: float32 [3, 16, 32, 8], P(None, 'cx', 'cy')
Inputs may be any that keep to these rules, and one draw needn't show every extreme that they name: pair_second indexes the owner's block of clusters extended by one cluster on every side (rows of 10 entries) and lies at most one cluster away from the slot's pair_first cluster in each direction; the pairs of one owner are distinct; slots from pair_count on hold such pairs too and are ignored. `pair_count`: some owners hold exactly 64 live pairs in every draw. `row_atom`: along the last dimension the atom numbers never fall, every atom has 1 to 32 functions.
All inputs are finite; a program needn't handle non-finite values.
Results may differ from a plain program's by a relative error of at most 0.0025.
Values may be sent and summed in bfloat16 or wider, within the bound.
No kernel may reach another device: no remote copies, remote signals or barrier semaphores. Data moves between devices by JAX's collectives and lax.ppermute only.
A program may use at most 192 MiB of HBM per device.

v0:
```python
import jax
import jax.numpy as jnp
from jax import lax
from jax.sharding import PartitionSpec as P

ATOMS = 8


def padded(cells, sides, width):
    for axis, dim in sides:
        count = lax.axis_size(axis)
        head = lax.slice_in_dim(cells, 0, width, axis=dim)
        tail = lax.slice_in_dim(cells, cells.shape[dim] - width, cells.shape[dim], axis=dim)
        cells = jnp.concatenate(
            [
                lax.ppermute(tail, axis, [(i, (i + 1) % count) for i in range(count)]),
                cells,
                lax.ppermute(head, axis, [((i + 1) % count, i) for i in range(count)]),
            ],
            axis=dim,
        )
    return cells


def weighted_stack(extended, occupation, energies):
    scaled = extended.astype(jnp.float32) * occupation
    first_half = scaled.astype(jnp.bfloat16)
    second_half = (scaled * energies).astype(jnp.bfloat16)
    return jnp.concatenate((first_half, second_half), axis=2)


def per_device(
    coeffs, occupation, energies, row_atom, pair_first, pair_second, pair_count, deriv_h, deriv_s
):
    highest = lax.Precision.HIGHEST
    width_x, width_y, basis_size, columns = coeffs.shape
    half_rows = row_atom.shape[2]
    local_count = width_x * width_y
    ext_y = width_y + 2
    ext_count = (width_x + 2) * ext_y
    row_offset = lax.axis_index("orb") * half_rows
    slot_count = pair_first.shape[2]
    all_occ, all_energy = (
        lax.all_gather(occupation, "orb", axis=0, tiled=True),
        lax.all_gather(energies, "orb", axis=0, tiled=True),
    )
    own_full = lax.all_gather(coeffs, "orb", axis=3, tiled=True)
    extended = padded(own_full, (("cx", 0), ("cy", 1)), 1)
    stacked = weighted_stack(extended, all_occ, all_energy)
    left_source = lax.dynamic_slice_in_dim(extended, row_offset, half_rows, 2)
    grad_h_all = deriv_h.reshape(slot_count, 3, half_rows, basis_size)
    grad_s_all = deriv_s.reshape(slot_count, 3, half_rows, basis_size)
    atoms_flat = row_atom.reshape(local_count, half_rows)
    left_flat = left_source.reshape(ext_count, left_source.shape[2], left_source.shape[3])
    stack_flat = stacked.reshape(ext_count, 2 * basis_size, stacked.shape[3])
    first_list = pair_first.reshape(slot_count)
    second_list = pair_second.reshape(slot_count)
    live_count = pair_count.reshape(())
    group_size = 8

    def visit(block_turn, totals):
        first_slot = block_turn * group_size
        first_ids = lax.dynamic_slice_in_dim(first_list, first_slot, group_size)
        second_ids = lax.dynamic_slice_in_dim(second_list, first_slot, group_size)
        live_mask = (first_slot + jnp.arange(group_size, dtype=jnp.int32) < live_count).astype(
            jnp.float32
        )
        row_ids = (first_ids // width_y + 1) * ext_y + first_ids % width_y + 1
        left_rows = jnp.take(left_flat, row_ids, axis=0)
        right_rows = jnp.take(stack_flat, second_ids, axis=0)
        products = jnp.einsum(
            "pmo,pno->pmn", left_rows, right_rows, preferred_element_type=jnp.float32
        )
        grad_h = lax.dynamic_slice_in_dim(grad_h_all, first_slot, group_size).astype(jnp.float32)
        grad_s = lax.dynamic_slice_in_dim(grad_s_all, first_slot, group_size).astype(jnp.float32)
        rowsum = jnp.sum(
            products[:, None, :, :basis_size] * grad_h - products[:, None, :, basis_size:] * grad_s,
            axis=3,
        )
        atom_ids = jnp.take(atoms_flat, first_ids, axis=0)
        atom_pick = (atom_ids[:, :, None] == jnp.arange(ATOMS, dtype=jnp.int32)).astype(jnp.float32)
        per_atom = (
            jnp.einsum("pcm,pma->pca", rowsum, atom_pick, precision=highest)
            * live_mask[:, None, None]
        )
        cluster_pick = (first_ids[:, None] == jnp.arange(local_count, dtype=jnp.int32)).astype(
            jnp.float32
        )
        return totals + jnp.einsum("pca,pl->cla", per_atom, cluster_pick, precision=highest)

    steps_needed = (live_count + group_size - 1) // group_size
    start_totals = jnp.zeros((3, local_count, ATOMS), jnp.float32)
    totals = lax.fori_loop(0, steps_needed, visit, start_totals)
    forces = lax.psum(-2.0 * totals, "orb")
    return forces.reshape(3, width_x, width_y, ATOMS)


def solution(mesh):
    return jax.shard_map(
        per_device,
        mesh=mesh,
        in_specs=(
            P("cx", "cy", None, "orb"),
            P("orb"),
            P("orb"),
            P("cx", "cy", "orb"),
            P("cx", "cy", None),
            P("cx", "cy", None),
            P("cx", "cy"),
            P("cx", "cy", None, None, "orb", None),
            P("cx", "cy", None, None, "orb", None),
        ),
        out_specs=P(None, "cx", "cy", None),
        check_vma=False,
    )
```

profile of v0, /device:TPU:15, one launch (start us, length us, event | category | flops | bytes accessed | tf_op | source)
XLA Modules:
  0.0 465.0 jit_solution(3508763258761499897)
XLA Ops:
  7.3 23.3 %all-gather.4.cloned.1.call-done = bf16[4,8,128,1024]{3,2,1,0:T(8,128)(2,1)} async-done(((bf16[4,8,128,512]{3,2,1,0:T(8,128)(2,1)}), bf16[4,8,128,1024]{3,2,1,0:T(8,128)(2,1)}) %all-gather.4.cloned.1.call-update) | async-done | bytes 8388624 | tf_op jit(solution)/shard_map/all_gather | solution.py:47
  34.8 45.6 %collective-permute-done = bf16[1,8,128,1024]{3,2,1,0:T(8,128)(2,1)S(1)} collective-permute-done((bf16[1,8,128,1024]{3,2,1,0:T(8,128)(2,1)S(1)}, bf16[1,8,128,1024]{3,2,1,0:T(8,128)(2,1)S(1)}, u32[]{:S(2)}, u32[]{:S(2)}) %collective-permute-start) | collective-permute-done | bytes 2097184 | tf_op jit(solution)/shard_map/ppermute | solution.py:16
  81.8 8.3 %constant_dynamic-update-slice_fusion.1 = bf16[6,8,128,1024]{3,2,1,0:T(8,128)(2,1)} fusion(bf16[6,8,128,1024]{3,2,1,0:T(8,128)(2,1)} %constant_dynamic-update-slice_fusion.2, bf16[4,8,128,1024]{3,2,1,0:T(8,128)(2,1)} %all-gather.4.cloned.1.call-done), kind=kLoop, calls=%fused_computation.46 | loop fusion | bytes 16777216
  90.2 36.5 %collective-permute-done.1 = bf16[1,8,128,1024]{3,2,1,0:T(8,128)(2,1)S(1)} collective-permute-done((bf16[1,8,128,1024]{3,2,1,0:T(8,128)(2,1)S(1)}, bf16[1,8,128,1024]{3,2,1,0:T(8,128)(2,1)S(1)}, u32[]{:S(2)}, u32[]{:S(2)}) %collective-permute-start.1) | collective-permute-done | bytes 2097184 | tf_op jit(solution)/shard_map/ppermute | solution.py:18
  137.1 29.1 %collective-permute-done.2 = bf16[6,1,128,1024]{3,2,1,0:T(8,128)(2,1)} collective-permute-done((bf16[6,1,128,1024]{3,2,1,0:T(8,128)(2,1)S(1)}, bf16[6,1,128,1024]{3,2,1,0:T(8,128)(2,1)}, u32[]{:S(2)}, u32[]{:S(2)}) %collective-permute-start.2) | collective-permute-done | bytes 1572896 | tf_op jit(solution)/shard_map/ppermute | solution.py:16
  166.3 33.7 %collective-permute-done.3 = bf16[6,1,128,1024]{3,2,1,0:T(8,128)(2,1)} collective-permute-done((bf16[6,1,128,1024]{3,2,1,0:T(8,128)(2,1)S(1)}, bf16[6,1,128,1024]{3,2,1,0:T(8,128)(2,1)}, u32[]{:S(2)}, u32[]{:S(2)}) %collective-permute-start.3) | collective-permute-done | bytes 1572896 | tf_op jit(solution)/shard_map/ppermute | solution.py:18
  200.0 13.4 %pad_maximum_fusion.1 = bf16[6,10,128,1024]{3,2,1,0:T(8,128)(2,1)} fusion(bf16[6,1,128,1024]{3,2,1,0:T(8,128)(2,1)} %collective-permute-done.3, bf16[6,8,128,1024]{3,2,1,0:T(8,128)(2,1)} %constant_dynamic-update-slice_fusion, bf16[6,1,128,1024]{3,2,1,0:T(8,128)(2,1)} %collective-permute-done.2), kind=kLoop, calls=%fused_computation.44 | loop fusion | flops 15728640 | bytes 31457280 | tf_op jit(solution)/shard_map/concatenate | solution.py:14
  213.4 7.9 %constant_dynamic-slice_fusion = bf16[6,10,64,1024]{3,2,1,0:T(8,128)(2,1)} fusion(bf16[6,10,128,1024]{3,2,1,0:T(8,128)(2,1)} %pad_maximum_fusion.1, s32[]{:T(128)S(6)} %select_n.84), kind=kLoop, calls=%fused_computation.49 | loop fusion | bytes 15728644 | tf_op jit(solution)/shard_map/dynamic_slice | solution.py:50
  221.3 19.9 %fusion.17 = (bf16[60,128,1024]{2,1,0:T(8,128)(2,1)}, bf16[60,128,1024]{2,1,0:T(8,128)(2,1)}) fusion(bf16[6,10,128,1024]{3,2,1,0:T(8,128)(2,1)} %pad_maximum_fusion.1, f32[1024]{0:T(1024)S(1)} %bitcast.38, f32[1024]{0:T(1024)S(1)} %bitcast.39), kind=kLoop, calls=%fused_computation.42 | loop fusion | flops 39321600 | bytes 47194112 | tf_op jit(solution)/shard_map/convert_element_type | solution.py:27
  241.2 21.1 %pad_maximum_fusion = bf16[60,256,1024]{2,1,0:T(8,128)(2,1)} fusion(bf16[60,128,1024]{2,1,0:T(8,128)(2,1)} %get-tuple-element.182, bf16[60,128,1024]{2,1,0:T(8,128)(2,1)} %get-tuple-element.181), kind=kLoop, calls=%fused_computation.39 | loop fusion | flops 62914560 | bytes 62914560 | tf_op jit(solution)/shard_map/concatenate | solution.py:29
  262.4 190.5 %while.12 = (s32[]{:T(128)}, f32[3,32,8]{1,2,0:T(8,128)S(1)}, s32[]{:T(128)}, s32[64]{0:T(128)S(1)}, bf16[60,64,1024]{2,1,0:T(8,128)(2,1)}, /*index=5*/s32[64]{0...) while((s32[]{:T(128)}, f32[3,32,8]{1,2,0:T(8,128)S(1)}, ...), condition=%wide.region_2.3_spmd, body=%wide.region_0.2_spmd.sunk | while | flops 272465472 | bytes 18657056 | solution.py:93
  263.9 3.8 gather_fusion.1
  267.7 12.7 %gather_fusion = bf16[8,256,1024]{2,1,0:T(8,128)(2,1)} fusion(bf16[60,256,1024]{2,1,0:T(8,128)(2,1)} %get-tuple-element.309, s32[1024]{0:T(1024)S(1)} %pad_clamp_fusion.6), kind=kCustom, calls=%fused_computation.1.clone.1 | custom fusion | bytes 8388640 | tf_op jit(solution)/shard_map/while/body/jit(_take)/gather | solution.py:70
  287.7 3.8 gather_fusion.1
  291.5 12.7 %gather_fusion = bf16[8,256,1024]{2,1,0:T(8,128)(2,1)} fusion(bf16[60,256,1024]{2,1,0:T(8,128)(2,1)} %get-tuple-element.309, s32[1024]{0:T(1024)S(1)} %pad_clamp_fusion.6), kind=kCustom, calls=%fused_computation.1.clone.1 | custom fusion | bytes 8388640 | tf_op jit(solution)/shard_map/while/body/jit(_take)/gather | solution.py:70
  311.5 3.8 gather_fusion.1
  315.4 12.7 %gather_fusion = bf16[8,256,1024]{2,1,0:T(8,128)(2,1)} fusion(bf16[60,256,1024]{2,1,0:T(8,128)(2,1)} %get-tuple-element.309, s32[1024]{0:T(1024)S(1)} %pad_clamp_fusion.6), kind=kCustom, calls=%fused_computation.1.clone.1 | custom fusion | bytes 8388640 | tf_op jit(solution)/shard_map/while/body/jit(_take)/gather | solution.py:70
  335.3 3.8 gather_fusion.1
  339.2 12.7 %gather_fusion = bf16[8,256,1024]{2,1,0:T(8,128)(2,1)} fusion(bf16[60,256,1024]{2,1,0:T(8,128)(2,1)} %get-tuple-element.309, s32[1024]{0:T(1024)S(1)} %pad_clamp_fusion.6), kind=kCustom, calls=%fused_computation.1.clone.1 | custom fusion | bytes 8388640 | tf_op jit(solution)/shard_map/while/body/jit(_take)/gather | solution.py:70
  363.0 12.7 %gather_fusion = bf16[8,256,1024]{2,1,0:T(8,128)(2,1)} fusion(bf16[60,256,1024]{2,1,0:T(8,128)(2,1)} %get-tuple-element.309, s32[1024]{0:T(1024)S(1)} %pad_clamp_fusion.6), kind=kCustom, calls=%fused_computation.1.clone.1 | custom fusion | bytes 8388640 | tf_op jit(solution)/shard_map/while/body/jit(_take)/gather | solution.py:70
  386.8 12.7 %gather_fusion = bf16[8,256,1024]{2,1,0:T(8,128)(2,1)} fusion(bf16[60,256,1024]{2,1,0:T(8,128)(2,1)} %get-tuple-element.309, s32[1024]{0:T(1024)S(1)} %pad_clamp_fusion.6), kind=kCustom, calls=%fused_computation.1.clone.1 | custom fusion | bytes 8388640 | tf_op jit(solution)/shard_map/while/body/jit(_take)/gather | solution.py:70
  410.6 12.7 %gather_fusion = bf16[8,256,1024]{2,1,0:T(8,128)(2,1)} fusion(bf16[60,256,1024]{2,1,0:T(8,128)(2,1)} %get-tuple-element.309, s32[1024]{0:T(1024)S(1)} %pad_clamp_fusion.6), kind=kCustom, calls=%fused_computation.1.clone.1 | custom fusion | bytes 8388640 | tf_op jit(solution)/shard_map/while/body/jit(_take)/gather | solution.py:70
  434.4 12.7 %gather_fusion = bf16[8,256,1024]{2,1,0:T(8,128)(2,1)} fusion(bf16[60,256,1024]{2,1,0:T(8,128)(2,1)} %get-tuple-element.309, s32[1024]{0:T(1024)S(1)} %pad_clamp_fusion.6), kind=kCustom, calls=%fused_computation.1.clone.1 | custom fusion | bytes 8388640 | tf_op jit(solution)/shard_map/while/body/jit(_take)/gather | solution.py:70
  452.9 5.3 %psum.7 = f32[3,4,8,8]{3,2,1,0:T(8,128)} all-reduce(f32[3,4,8,8]{3,2,1,0:T(8,128)S(1)} %bitcast.37), channel_id=1, replica_groups=mesh['cx'=4,'cy'=4,'orb'=2] {'orb'}, use_global_device_ids=true, to_apply=%region_3.4 | all-reduce | flops 768 | bytes 6144 | tf_op jit(solution)/shard_map/psum | solution.py:94
  (149 shorter events, 89.0 us)
Async XLA Ops:
  6.5 24.1 %all-gather.4.cloned.1.call-start = ((), (), s32[]{:S(2)}) async-start(), calls=%async_computation | async-start | bytes 12582912 | tf_op jit(solution)/shard_map/all_gather | solution.py:47
  33.3 47.1 %collective-permute-start = (bf16[1,8,128,1024]{3,2,1,0:T(8,128)(2,1)S(1)}, bf16[1,8,128,1024]{3,2,1,0:T(8,128)(2,1)S(1)}, u32[]{:S(2)}, u32[]{:S(2)}) collective-permute-start(bf16[1,8,128,1024]{3,2,1,0:T(8,128)(2,1)S(1)} %get-tuple-element.186), channel_id=1, source_target_pairs={{0,8},{8,16},{16,24},{24,0},{1,9},{9,17},{17,25},{25,1},{2,10},{10... | collective-permute-start | bytes 6291464 | tf_op jit(solution)/shard_map/ppermute | solution.py:16
  34.5 92.2 %collective-permute-start.1 = (bf16[1,8,128,1024]{3,2,1,0:T(8,128)(2,1)S(1)}, bf16[1,8,128,1024]{3,2,1,0:T(8,128)(2,1)S(1)}, u32[]{:S(2)}, u32[]{:S(2)}) collective-permute-start(bf16[1,8,128,1024]{3,2,1,0:T(8,128)(2,1)S(1)} %get-tuple-element.185), channel_id=1, source_target_pairs={{8,0},{16,8},{24,16},{0,24},{9,1},{17,9},{25,17},{1,25},{10,2},{18... | collective-permute-start | bytes 6291464 | tf_op jit(solution)/shard_map/ppermute | solution.py:18
  81.8 51.0 %copy-start.3 = (f32[512]{0:T(512)S(1)}, f32[512]{0:T(512)}, u32[]{:S(2)}) copy-start(f32[512]{0:T(512)} %param.12) | copy-start | bytes 6148
  81.8 53.5 %copy-start.4 = (f32[512]{0:T(512)S(1)}, f32[512]{0:T(512)}, u32[]{:S(2)}) copy-start(f32[512]{0:T(512)} %param.13) | copy-start | bytes 6148
  130.6 35.6 %collective-permute-start.2 = (bf16[6,1,128,1024]{3,2,1,0:T(8,128)(2,1)S(1)}, bf16[6,1,128,1024]{3,2,1,0:T(8,128)(2,1)}, u32[]{:S(2)}, u32[]{:S(2)}) collective-permute-start(bf16[6,1,128,1024]{3,2,1,0:T(8,128)(2,1)S(1)} %get-tuple-element.183), channel_id=1, source_target_pairs={{0,2},{2,4},{4,6},{6,0},{1,3},{3,5},{5,7},{7,1},{8,10},{10,12},{12... | collective-permute-start | bytes 4718600 | tf_op jit(solution)/shard_map/ppermute | solution.py:16
  130.7 69.2 %collective-permute-start.3 = (bf16[6,1,128,1024]{3,2,1,0:T(8,128)(2,1)S(1)}, bf16[6,1,128,1024]{3,2,1,0:T(8,128)(2,1)}, u32[]{:S(2)}, u32[]{:S(2)}) collective-permute-start(bf16[6,1,128,1024]{3,2,1,0:T(8,128)(2,1)S(1)} %get-tuple-element.184), channel_id=1, source_target_pairs={{2,0},{4,2},{6,4},{0,6},{3,1},{5,3},{7,5},{1,7},{10,8},{12,10},{14... | collective-permute-start | bytes 4718600 | tf_op jit(solution)/shard_map/ppermute | solution.py:18
  241.2 21.1 %copy-start = (s32[4,8,64]{2,1,0:T(8,128)S(1)}, s32[4,8,64]{2,1,0:T(8,128)}, u32[]{:S(2)}) copy-start(s32[4,8,64]{2,1,0:T(8,128)} %param.14) | copy-start | bytes 24580
  241.2 21.2 %copy-start.1 = (s32[1,1,64]{2,1,0:T(1,128)S(1)}, s32[1,1,64]{2,1,0:T(1,128)}, u32[]{:S(2)}) copy-start(s32[1,1,64]{2,1,0:T(1,128)} %param.15) | copy-start | bytes 772
  241.2 21.2 %copy-start.2 = (s32[1,1,64]{2,1,0:T(1,128)S(1)}, s32[1,1,64]{2,1,0:T(1,128)}, u32[]{:S(2)}) copy-start(s32[1,1,64]{2,1,0:T(1,128)} %param.16) | copy-start | bytes 772
Sparse Core Ops, SparseCore 0:
  8.9 21.6 all-gather.3
where the time goes:
time: 468 us; the launch traced here: 465 us
  waiting for transfers between devices  169 us (36%)
  local copies, waits for them, and re-layouts  162 us (35%)
  other arithmetic  73 us (16%)
  matrix products  33.3 us (7%)
  between operations  14.1 us (3%)
  blocking collectives  9.56 us (2%)
    gather x8, local copies, waits for them, and re-layouts, visit(): right_rows = jnp.take(stack_flat, second_ids, axis=0)  102 us
    ppermute x2, waiting for transfers between devices, padded(): lax.ppermute(tail, axis, [(i, (i + 1) % count) for i in range(count)])  74.7 us
    ppermute x2, waiting for transfers between devices, padded(): lax.ppermute(head, axis, [((i + 1) % count, i) for i in range(count)])  70.2 us
    gather x8, local copies, waits for them, and re-layouts, visit(): left_rows = jnp.take(left_flat, row_ids, axis=0)  30.8 us
    dot_general x8, matrix products, visit(): jnp.einsum('pmo,pno->pmn', left_rows, right_rows, preferred_element_type=...  29.2 us
    all_gather x1, waiting for transfers between devices, per_device(): own_full = lax.all_gather(coeffs, 'orb', axis=3, tiled=True)  23.3 us
    concatenate x1, other arithmetic, weighted_stack(): return jnp.concatenate((first_half, second_half), axis=2)  21.1 us
    convert_element_type x1, other arithmetic, weighted_stack(): first_half = scaled.astype(jnp.bfloat16)  19.9 us
  transfers between devices with their start and end apart: 5, of which 5 were waited for; matrix products, arithmetic and copies ran while one was open for 2% of the time, Pallas kernels for 0%

commit v1 on v0

v1 whole, which is shorter than its diff:
```python
import functools

import jax
import jax.numpy as jnp
from jax import lax
from jax.experimental import pallas as pl
from jax.experimental.pallas import tpu as pltpu
from jax.sharding import PartitionSpec as P

ATOMS = 8
RING = 8
ANY = pl.BlockSpec(memory_space=pl.ANY)
SMEM = pl.BlockSpec(memory_space=pltpu.SMEM)
VMEM = pl.BlockSpec(memory_space=pltpu.VMEM)


def shift(cells, axis, step):
    count = lax.axis_size(axis)
    return lax.ppermute(cells, axis, [(i, (i + step) % count) for i in range(count)])


def pair_term(left, right, occ, energy, atoms, grad):
    scaled = right.astype(jnp.float32) * occ
    weights = jnp.concatenate(
        (scaled.astype(jnp.bfloat16), (scaled * energy).astype(jnp.bfloat16)), axis=0
    )
    both = lax.dot_general(
        left, weights, (((1,), (1,)), ((), ())), preferred_element_type=jnp.float32
    )
    basis = right.shape[0]
    density, weighted = both[:, :basis], both[:, basis:]
    terms = jnp.concatenate(
        [
            density * grad(0, c).astype(jnp.float32) - weighted * grad(1, c).astype(jnp.float32)
            for c in range(3)
        ],
        axis=1,
    )
    high = terms.astype(jnp.bfloat16)
    low = (terms - high.astype(jnp.float32)).astype(jnp.bfloat16)
    pick = (lax.broadcasted_iota(jnp.int32, (ATOMS, basis), 0) == atoms).astype(jnp.bfloat16)
    return lax.dot_general(
        jnp.concatenate((pick, pick), axis=1),
        jnp.concatenate((high, low), axis=0),
        (((1,), (0,)), ((), ())),
        preferred_element_type=jnp.float32,
    )


def sort_slots(dims, second, count, lists):
    width_x, width_y, slots = dims
    for k in range(3):
        lists[3 * slots + k] = 0

    def place(s, carry):
        g = second[s]
        gx, gy = g // (width_y + 2), g % (width_y + 2)
        inside_x = jnp.logical_and(gx >= 1, gx <= width_x)
        inside_y = jnp.logical_and(gy >= 1, gy <= width_y)
        stage = jnp.where(inside_x, jnp.where(inside_y, 0, 1), 2)
        used = lists[3 * slots + stage]
        lists[stage * slots + used] = s
        lists[3 * slots + stage] = used + 1
        return carry

    lax.fori_loop(0, count, place, 0)


def stage_body(
    dims, stage, first, second, half, lists, coeffs, rims, grads, occ, energy, atoms, acc, scratch
):
    width_x, width_y, slots = dims
    left_ring, right_ring, grad_ring, sems = scratch
    half_rows = grads[0].shape[2]
    number = lists[3 * slots + stage]

    def grad_copies(s, r):
        out = []
        for kind in range(2):
            for part in range(2):
                out.append(
                    pltpu.make_async_copy(
                        grads[2 * kind + part].at[s],
                        grad_ring.at[r, kind, :, pl.ds(part * half_rows, half_rows), :],
                        sems.at[r, 2 * kind + part],
                    )
                )
        return out

    def left_copies(s, r):
        own = first[s]
        return [
            pltpu.make_async_copy(
                coeffs.at[own, pl.ds(pl.multiple_of(part * half_rows, half_rows), half_rows)],
                left_ring.at[r, pl.ds(place * half_rows, half_rows)],
                sems.at[r, 4 + place],
            )
            for place, part in enumerate((half, 1 - half))
        ]

    def right_copy(source, r):
        return pltpu.make_async_copy(source, right_ring.at[r], sems.at[r, 6])

    def start(i):
        s = lists[stage * slots + i]
        r = lax.rem(i, RING)
        g = second[s]
        gx, gy = g // (width_y + 2) - 1, g % (width_y + 2) - 1
        if stage == 0:
            right_copy(coeffs.at[gx * width_y + gy], r).start()
        elif stage == 1:
            for side, rim in enumerate(rims):

                @pl.when((gy < 0) == (side == 0))
                def _():
                    right_copy(rim.at[gx], r).start()
        else:
            row = (gx > 0).astype(jnp.int32)
            low_edge, high_edge, low_mid, high_mid, low_corner, high_corner = rims
            at_edge = jnp.logical_or(gy == 0, gy == width_y - 1)
            outside = jnp.logical_or(gy < 0, gy >= width_y)
            inner = jnp.logical_not(jnp.logical_or(at_edge, outside))
            for side, edge, mid, corner in (
                (0, low_edge, low_mid, low_corner),
                (1, high_edge, high_mid, high_corner),
            ):
                here = row == side

                @pl.when(jnp.logical_and(here, at_edge))
                def _():
                    right_copy(edge.at[(gy > 0).astype(jnp.int32)], r).start()

                @pl.when(jnp.logical_and(here, inner))
                def _():
                    right_copy(mid.at[gy - 1], r).start()

                @pl.when(jnp.logical_and(outside, (gy < 0) == (side == 0)))
                def _():
                    right_copy(corner.at[row], r).start()

        for copy in left_copies(s, r) + grad_copies(s, r):
            copy.start()

    def begin(i, carry):
        start(i)
        return carry

    lax.fori_loop(0, jnp.minimum(number, RING - 1), begin, 0)

    def visit(i, carry):
        @pl.when(i + RING - 1 < number)
        def _():
            start(i + RING - 1)

        s = lists[stage * slots + i]
        r = lax.rem(i, RING)
        own = first[s]
        right_copy(coeffs.at[0], r).wait()
        for copy in left_copies(s, r) + grad_copies(s, r):
            copy.wait()
        acc[own] += pair_term(
            left_ring[r],
            right_ring[r],
            occ[...],
            energy[...],
            atoms[pl.ds(own, 1), :],
            lambda kind, c: grad_ring[r, kind, c],
        )
        return carry

    lax.fori_loop(0, number, visit, 0)


def own_kernel(
    dims, first, second, meta, coeffs, gh, gh2, gs, gs2, occ, energy, atoms, acc, lists, *scratch
):
    acc[...] = jnp.zeros_like(acc)
    sort_slots(dims, second, meta[0], lists)
    stage_body(
        dims, 0, first, second, meta[1], lists, coeffs, (), (gh, gh2, gs, gs2), occ, energy, atoms,
        acc, scratch,
    )


def rim_kernel(
    dims, stage, rim_count, first, second, meta, lists, coeffs, gh, gh2, gs, gs2, occ, energy,
    atoms, before, *rest
):
    rims, out, scratch = rest[:rim_count], rest[rim_count], rest[rim_count + 1 :]
    if stage == 1:
        acc = out
    else:
        acc, scratch = scratch[-1], scratch[:-1]
    acc[...] = before[...]
    stage_body(
        dims, stage, first, second, meta[1], lists, coeffs, rims, (gh, gh2, gs, gs2), occ, energy,
        atoms, acc, scratch,
    )
    if stage == 2:
        basis = atoms.shape[1]
        for c in range(3):
            out[c] = -2.0 * jnp.sum(acc[:, :, c * basis : (c + 1) * basis], axis=2)


def per_device(
    coeffs, occupation, energies, row_atom, pair_first, pair_second, pair_count, deriv_h, deriv_s
):
    width_x, width_y, basis, columns = coeffs.shape
    half_rows = row_atom.shape[2]
    local = width_x * width_y
    slots = pair_first.shape[2]
    dims = (width_x, width_y, slots)

    edge_pair = jnp.stack((coeffs[:, 0], coeffs[:, width_y - 1]), axis=1)
    low_edge = shift(edge_pair[width_x - 1], "cx", 1)
    high_edge = shift(edge_pair[0], "cx", -1)
    low_mid = shift(coeffs[width_x - 1, 1 : width_y - 1], "cx", 1)
    high_mid = shift(coeffs[0, 1 : width_y - 1], "cx", -1)
    low_side = shift(edge_pair[:, 1], "cy", 1)
    high_side = shift(edge_pair[:, 0], "cy", -1)
    low_corner = shift(jnp.stack((low_edge[1], high_edge[1])), "cy", 1)
    high_corner = shift(jnp.stack((low_edge[0], high_edge[0])), "cy", -1)

    grad_h = deriv_h.reshape(slots, 3, half_rows, basis)
    grad_s = deriv_s.reshape(slots, 3, half_rows, basis)
    grads = (grad_h, shift(grad_h, "orb", 1), grad_s, shift(grad_s, "orb", 1))
    atoms_own = row_atom.reshape(local, half_rows)
    atoms = jnp.concatenate((atoms_own, shift(atoms_own, "orb", 1)), axis=1)

    flat = coeffs.reshape(local, basis, columns)
    first, second = pair_first.reshape(slots), pair_second.reshape(slots)
    meta = jnp.stack((pair_count.reshape(()), lax.axis_index("orb").astype(jnp.int32)))
    occ, energy = occupation.reshape(1, columns), energies.reshape(1, columns)

    scratch = [
        pltpu.VMEM((RING, basis, columns), jnp.bfloat16),
        pltpu.VMEM((RING, basis, columns), jnp.bfloat16),
        pltpu.VMEM((RING, 2, 3, basis, basis), jnp.bfloat16),
        pltpu.SemaphoreType.DMA((RING, 7)),
    ]
    acc_shape = jax.ShapeDtypeStruct((local, ATOMS, 3 * basis), jnp.float32)
    list_shape = jax.ShapeDtypeStruct((3 * slots + 8,), jnp.int32)
    params = pltpu.CompilerParams(vmem_limit_bytes=24 * 1024 * 1024)

    def cost(share):
        pairs = int(slots * share)
        return pl.CostEstimate(
            flops=pairs * basis * 2 * basis * columns * 2,
            bytes_accessed=pairs * 2 * (2 * basis * columns + 6 * basis * basis),
            transcendentals=0,
        )

    acc, lists = pl.pallas_call(
        functools.partial(own_kernel, dims),
        out_shape=(acc_shape, list_shape),
        in_specs=[SMEM] * 3 + [ANY] * 5 + [VMEM] * 3,
        out_specs=(VMEM, SMEM),
        scratch_shapes=scratch,
        compiler_params=params,
        cost_estimate=cost(0.75),
    )(first, second, meta, flat, *grads, occ, energy, atoms)
    for stage, rims, out_shape in (
        (1, (low_side, high_side), acc_shape),
        (
            2,
            (low_edge, high_edge, low_mid, high_mid, low_corner, high_corner),
            jax.ShapeDtypeStruct((3, local, ATOMS), jnp.float32),
        ),
    ):
        acc = pl.pallas_call(
            functools.partial(rim_kernel, dims, stage, len(rims)),
            out_shape=out_shape,
            in_specs=[SMEM] * 4 + [ANY] * 5 + [VMEM] * 4 + [ANY] * len(rims),
            out_specs=VMEM,
            scratch_shapes=scratch
            + ([pltpu.VMEM(acc_shape.shape, jnp.float32)] if stage == 2 else []),
            compiler_params=params,
            cost_estimate=cost(0.15),
        )(first, second, meta, lists, flat, *grads, occ, energy, atoms, acc, *rims)
    return lax.psum(acc, "orb").reshape(3, width_x, width_y, ATOMS)


def solution(mesh):
    return jax.shard_map(
        per_device,
        mesh=mesh,
        in_specs=(
            P("cx", "cy", None, "orb"),
            P("orb"),
            P("orb"),
            P("cx", "cy", "orb"),
            P("cx", "cy", None),
            P("cx", "cy", None),
            P("cx", "cy"),
            P("cx", "cy", None, None, "orb", None),
            P("cx", "cy", None, None, "orb", None),
        ),
        out_specs=P(None, "cx", "cy", None),
        check_vma=False,
    )
```

time: 468 us -> 90.6 us (0.19)
  the two profiles are of different devices: /device:TPU:15 before, /device:TPU:5 now
where the time goes in v1:
time: 90.6 us; the launch traced here: 90.2 us
  Pallas kernels  55.1 us (61%)
  waiting for transfers between devices  10.7 us (12%)
  starting transfers between devices  9.53 us (11%)
  blocking collectives  6.85 us (8%)
  local copies, waits for them, and re-layouts  5.88 us (6%)
  other arithmetic  1.09 us (1%)
  between operations  0.97 us (1%)
    pallas_call x1, Pallas kernels, per_device(): pl.pallas_call(functools.partial(own_kernel, dims), out_shape=(acc_shape,...  40.2 us
    pallas_call x2, Pallas kernels, per_device(): pl.pallas_call(functools.partial(rim_kernel, dims, stage, len(rims)), out...  14.9 us
    ppermute x11, waiting for transfers between devices, shift(): lax.ppermute(cells, axis, [(i, (i + step) % count) for i in range(count)])  10.7 us
    ppermute x11, starting transfers between devices, shift(): lax.ppermute(cells, axis, [(i, (i + step) % count) for i in range(count)])  9.53 us
    psum x1, blocking collectives, per_device(): return lax.psum(acc, 'orb').reshape(3, width_x, width_y, ATOMS)  6.85 us
    slice x1, local copies, waits for them, and re-layouts, per_device(): edge_pair = jnp.stack((coeffs[:, 0], coeffs[:, width_y - 1]), axis=1)  2.46 us
    unnamed x16, local copies, waits for them, and re-layouts  1.91 us
  transfers between devices with their start and end apart: 11, of which 2 were waited for; matrix products, arithmetic and copies ran while one was open for 6% of the time, Pallas kernels for 48%

profile of v1, /device:TPU:5, one launch (start us, length us, event | category | flops | bytes accessed | tf_op | source)
XLA Modules:
  0.0 90.2 jit_solution(2370117142834329646)
XLA Ops:
  0.0 0.7 collective-permute-start
  0.7 0.0 collective-permute-start.1
  0.7 0.5 collective-permute-start.2
  1.2 2.5 %fusion.1 = (bf16[4,1,128,512]{3,2,1,0:T(8,128)(2,1)S(1)}, bf16[4,128,512]{2,1,0:T(8,128)(2,1)}, bf16[4,128,512]{2,1,0:T(8,128)(2,1)}, bf16[4,1,128,512]{3,2,1,0:T(8,128)(2,1)S(1)}) fusion(bf16[4,8,128,512]{3,2,1,0:T(8,128)(2,1)} %param.9), kind=kLoop, calls=%fused_computation.11 | loop fusion | bytes 3145728 | tf_op jit(solution)/shard_map/slice | solution.py:214
  3.7 1.2 %collective-permute-start.3 = (bf16[4,128,512]{2,1,0:T(8,128)(2,1)}, bf16[4,128,512]{2,1,0:T(8,128)(2,1)}, u32[]{:S(2)}, u32[]{:S(2)}) collective-permute-start(bf16[4,128,512]{2,1,0:T(8,128)(2,1)} %get-tuple-element.12), channel_id=1, source_target_pairs={{0,2},{2,4},{4,6},{6,0},{1,3},{3,5},{5,7},{7,1},{8,10},{10,12},{12... | collective-permute-start | bytes 1572872 | tf_op jit(solution)/shard_map/ppermute | solution.py:19
  4.9 0.0 copy-start.6
  4.9 0.9 fusion
  5.8 1.3 %collective-permute-start.5 = (bf16[2,128,512]{2,1,0:T(8,128)(2,1)}, bf16[2,128,512]{2,1,0:T(8,128)(2,1)S(1)}, u32[]{:S(2)}, u32[]{:S(2)}) collective-permute-start(bf16[2,128,512]{2,1,0:T(8,128)(2,1)} %get-tuple-element.16), channel_id=1, source_target_pairs={{0,8},{8,16},{16,24},{24,0},{1,9},{9,17},{17,25},{25,1},{2,10},{10... | collective-permute-start | bytes 786440 | tf_op jit(solution)/shard_map/ppermute | solution.py:19
  7.9 0.1 pad_add_fusion.1.meta
  8.0 2.0 %collective-permute-start.6 = (bf16[2,128,512]{2,1,0:T(8,128)(2,1)}, bf16[2,128,512]{2,1,0:T(8,128)(2,1)S(1)}, u32[]{:S(2)}, u32[]{:S(2)}) collective-permute-start(bf16[2,128,512]{2,1,0:T(8,128)(2,1)} %get-tuple-element.15), channel_id=1, source_target_pairs={{0,24},{8,0},{16,8},{24,16},{1,25},{9,1},{17,9},{25,17},{2,26},{10... | collective-permute-start | bytes 786440 | tf_op jit(solution)/shard_map/ppermute | solution.py:19
  10.0 1.5 %slice_bitcast_fusion = (bf16[6,128,512]{2,1,0:T(8,128)(2,1)S(1)}, bf16[6,128,512]{2,1,0:T(8,128)(2,1)S(1)}) fusion(bf16[4,8,128,512]{3,2,1,0:T(8,128)(2,1)} %param.9), kind=kLoop, calls=%fused_computation | loop fusion | bytes 3145728 | tf_op jit(solution)/shard_map/squeeze | solution.py:218
  11.5 4.1 %collective-permute-done.5.rest_0_ = bf16[2,128,512]{2,1,0:T(8,128)(2,1)S(1)} collective-permute-done((bf16[2,128,512]{2,1,0:T(8,128)(2,1)}, bf16[2,128,512]{2,1,0:T(8,128)(2,1)S(1)}, u32[]{:S(2)}, u32[]{:S(2)}) %collective-permute-start.5) | collective-permute-done | bytes 262176 | tf_op jit(solution)/shard_map/ppermute | solution.py:19
  15.6 6.6 %collective-permute-done.6.rest_1_ = bf16[2,128,512]{2,1,0:T(8,128)(2,1)S(1)} collective-permute-done((bf16[2,128,512]{2,1,0:T(8,128)(2,1)}, bf16[2,128,512]{2,1,0:T(8,128)(2,1)S(1)}, u32[]{:S(2)}, u32[]{:S(2)}) %collective-permute-start.6) | collective-permute-done | bytes 262176 | tf_op jit(solution)/shard_map/ppermute | solution.py:19
  22.2 0.2 collective-permute-start.8
  22.4 1.2 %collective-permute-start.4 = (bf16[4,128,512]{2,1,0:T(8,128)(2,1)}, bf16[4,128,512]{2,1,0:T(8,128)(2,1)S(1)}, u32[]{:S(2)}, u32[]{:S(2)}) collective-permute-start(bf16[4,128,512]{2,1,0:T(8,128)(2,1)} %get-tuple-element.13), channel_id=1, source_target_pairs={{0,6},{2,0},{4,2},{6,4},{1,7},{3,1},{5,3},{7,5},{8,14},{10,8},{12,... | collective-permute-start | bytes 1572872 | tf_op jit(solution)/shard_map/ppermute | solution.py:19
  23.7 0.4 collective-permute-start.9
  24.1 2.1 %collective-permute-start.10 = (bf16[2,128,512]{2,1,0:T(8,128)(2,1)S(1)}, bf16[2,128,512]{2,1,0:T(8,128)(2,1)S(1)}, u32[]{:S(2)}, u32[]{:S(2)}) collective-permute-start(bf16[2,128,512]{2,1,0:T(8,128)(2,1)S(1)} %pad_maximum_fusion.2), channel_id=1, source_target_pairs={{0,6},{2,0},{4,2},{6,4},{1,7},{3,1},{5,3},{7,5},{8,14},{10,8},{12,... | collective-permute-start | bytes 786440 | tf_op jit(solution)/shard_map/ppermute | solution.py:19
  26.1 0.1 pad_add_fusion.atoms
  26.2 0.0 copy-start.2
  26.3 1.9 %copy-done.2 = bf16[1,1,64,3,64,128]{5,4,3,2,1,0:T(8,128)(2,1)S(1)} copy-done((bf16[1,1,64,3,64,128]{5,4,3,2,1,0:T(8,128)(2,1)S(1)}, bf16[1,1,64,3,64,128]{5,4,3,2,1,0:T(8,128)(2,1)}, u32[]{:S(2)}) %copy-start.2) | copy-done | bytes 3145752
  28.1 40.2 %shard_map.91 = (f32[32,8,384]{2,1,0:T(8,128)S(1)}, s32[200]{0:T(256)S(1)}) custom-call(s32[64]{0:T(128)S(1)} %bitcast.42, s32[64]{0:T(128)S(1)} %bitcast.45, s32[2]{0:T(128)S(1)} %pad_add_fusion.1.meta, bf16[32,128,512]{2,1,0:T(8,128)(2,1)S(1)} %bitcast.24, bf16[64,3,64,128]{3,2,1,0:T(8,128)(2,1)S(1)} %bitcast.28, ...), custom_call_target="tpu_custom_call" | custom-call | flops 1610612736 | bytes 22020096 | tf_op jit(solution)/shard_map/pallas_call | solution.py:253
  68.4 3.1 %shard_map.92.before = f32[32,8,384]{2,1,0:T(8,128)S(1)} custom-call(s32[64]{0:T(128)S(1)} %bitcast.43, s32[64]{0:T(128)S(1)} %bitcast.46, s32[2]{0:T(128)S(1)} %pad_add_fusion.1.meta, s32[200]{0:T(256)S(1)} %get-tuple-element.7.lists, bf16[32,128,512]{2,1,0:T(8,128)(2,1)S(1)} %bitcast.25, bf16[64,3,64,128]{3,2,1,0:T(8,128)(2,1)S(1)} %bitcast.29, ...), custom_call_target="tpu_custom_call" | custom-call | flops 301989888 | bytes 4128768 | tf_op jit(solution)/shard_map/pallas_call | solution.py:270
  71.5 11.8 %shard_map.93 = f32[3,32,8]{2,1,0:T(8,128)S(1)} custom-call(s32[64]{0:T(128)S(1)} %bitcast.44, s32[64]{0:T(128)S(1)} %bitcast.47, s32[2]{0:T(128)S(1)} %pad_add_fusion.1.meta, s32[200]{0:T(256)S(1)} %get-tuple-element.7.lists, bf16[32,128,512]{2,1,0:T(8,128)(2,1)S(1)} %bitcast.26, bf16[64,3,64,128]{3,2,1,0:T(8,128)(2,1)S(1)} %bitcast.30, ...), custom_call_target="tpu_custom_call" | custom-call | flops 301989888 | bytes 4128768 | tf_op jit(solution)/shard_map/pallas_call | solution.py:270
  83.3 6.8 %psum.7 = f32[3,4,8,8]{3,2,1,0:T(8,128)} all-reduce(f32[3,4,8,8]{3,2,1,0:T(8,128)S(1)} %bitcast.35), channel_id=1, replica_groups=mesh['cx'=4,'cy'=4,'orb'=2] {'orb'}, use_global_device_ids=true, to_apply=%region_0.0 | all-reduce | flops 768 | bytes 6144 | tf_op jit(solution)/shard_map/psum | solution.py:280
  (27 shorter events, 0.1 us)
Async XLA Ops:
  0.0 23.7 %collective-permute-start = (bf16[64,3,64,128]{3,2,1,0:T(8,128)(2,1)}, bf16[64,3,64,128]{3,2,1,0:T(8,128)(2,1)}, u32[]{:S(2)}, u32[]{:S(2)}) collective-permute-start(bf16[64,3,64,128]{3,2,1,0:T(8,128)(2,1)} %bitcast.27), channel_id=1, source_target_pairs={{0,1},{1,0},{2,3},{3,2},{4,5},{5,4},{6,7},{7,6},{8,9},{9,8},{10,11... | collective-permute-start | bytes 9437192 | tf_op jit(solution)/shard_map/ppermute | solution.py:19
  0.7 23.4 %collective-permute-start.1 = (bf16[64,3,64,128]{3,2,1,0:T(8,128)(2,1)}, bf16[64,3,64,128]{3,2,1,0:T(8,128)(2,1)}, u32[]{:S(2)}, u32[]{:S(2)}) collective-permute-start(bf16[64,3,64,128]{3,2,1,0:T(8,128)(2,1)} %bitcast.31), channel_id=1, source_target_pairs={{0,1},{1,0},{2,3},{3,2},{4,5},{5,4},{6,7},{7,6},{8,9},{9,8},{10,11... | collective-permute-start | bytes 9437192 | tf_op jit(solution)/shard_map/ppermute | solution.py:19
  0.7 7.3 %collective-permute-start.2 = (s32[32,64]{1,0:T(8,128)}, s32[32,64]{1,0:T(8,128)S(1)}, u32[]{:S(2)}, u32[]{:S(2)}) collective-permute-start(s32[32,64]{1,0:T(8,128)} %bitcast.48), channel_id=1, source_target_pairs={{0,1},{1,0},{2,3},{3,2},{4,5},{5,4},{6,7},{7,6},{8,9},{9,8},{10,11... | collective-permute-start | bytes 24584 | tf_op jit(solution)/shard_map/ppermute | solution.py:19
  1.2 25.0 %copy-start.1 = (bf16[1,1,64,3,64,128]{5,4,3,2,1,0:T(8,128)(2,1)S(1)}, bf16[1,1,64,3,64,128]{5,4,3,2,1,0:T(8,128)(2,1)}, u32[]{:S(2)}) copy-start(bf16[1,1,64,3,64,128]{5,4,3,2,1,0:T(8,128)(2,1)} %param.16) | copy-start | bytes 9437188
  3.7 18.7 %collective-permute-start.3 = (bf16[4,128,512]{2,1,0:T(8,128)(2,1)}, bf16[4,128,512]{2,1,0:T(8,128)(2,1)}, u32[]{:S(2)}, u32[]{:S(2)}) collective-permute-start(bf16[4,128,512]{2,1,0:T(8,128)(2,1)} %get-tuple-element.12), channel_id=1, source_target_pairs={{0,2},{2,4},{4,6},{6,0},{1,3},{3,5},{5,7},{7,1},{8,10},{10,12},{12... | collective-permute-start | bytes 1572872 | tf_op jit(solution)/shard_map/ppermute | solution.py:19
  4.9 21.3 %copy-start.7 = (s32[4,8,64]{2,1,0:T(8,128)S(1)}, s32[4,8,64]{2,1,0:T(8,128)}, u32[]{:S(2)}) copy-start(s32[4,8,64]{2,1,0:T(8,128)} %param.12) | copy-start | bytes 24580
  4.9 21.3 %copy-start.3 = (f32[512]{0:T(512)S(1)}, f32[512]{0:T(512)}, u32[]{:S(2)}) copy-start(f32[512]{0:T(512)} %param.10) | copy-start | bytes 6148
  4.9 21.3 %copy-start.4 = (f32[512]{0:T(512)S(1)}, f32[512]{0:T(512)}, u32[]{:S(2)}) copy-start(f32[512]{0:T(512)} %param.11) | copy-start | bytes 6148
  4.9 21.3 %copy-start.5 = (s32[1,1,64]{2,1,0:T(1,128)S(1)}, s32[1,1,64]{2,1,0:T(1,128)}, u32[]{:S(2)}) copy-start(s32[1,1,64]{2,1,0:T(1,128)} %param.13) | copy-start | bytes 772
  4.9 21.4 %copy-start.6 = (s32[1,1,64]{2,1,0:T(1,128)S(1)}, s32[1,1,64]{2,1,0:T(1,128)}, u32[]{:S(2)}) copy-start(s32[1,1,64]{2,1,0:T(1,128)} %param.14) | copy-start | bytes 772
  5.8 9.8 %collective-permute-start.5 = (bf16[2,128,512]{2,1,0:T(8,128)(2,1)}, bf16[2,128,512]{2,1,0:T(8,128)(2,1)S(1)}, u32[]{:S(2)}, u32[]{:S(2)}) collective-permute-start(bf16[2,128,512]{2,1,0:T(8,128)(2,1)} %get-tuple-element.16), channel_id=1, source_target_pairs={{0,8},{8,16},{16,24},{24,0},{1,9},{9,17},{17,25},{25,1},{2,10},{10... | collective-permute-start | bytes 786440 | tf_op jit(solution)/shard_map/ppermute | solution.py:19
  7.1 19.2 %copy-start = (bf16[4,8,128,512]{3,2,1,0:T(8,128)(2,1)S(1)}, bf16[4,8,128,512]{3,2,1,0:T(8,128)(2,1)}, u32[]{:S(2)}) copy-start(bf16[4,8,128,512]{3,2,1,0:T(8,128)(2,1)} %param.9) | copy-start | bytes 12582916
  8.0 14.2 %collective-permute-start.6 = (bf16[2,128,512]{2,1,0:T(8,128)(2,1)}, bf16[2,128,512]{2,1,0:T(8,128)(2,1)S(1)}, u32[]{:S(2)}, u32[]{:S(2)}) collective-permute-start(bf16[2,128,512]{2,1,0:T(8,128)(2,1)} %get-tuple-element.15), channel_id=1, source_target_pairs={{0,24},{8,0},{16,8},{24,16},{1,25},{9,1},{17,9},{25,17},{2,26},{10... | collective-permute-start | bytes 786440 | tf_op jit(solution)/shard_map/ppermute | solution.py:19
  15.6 55.9 %collective-permute-start.7 = (bf16[6,128,512]{2,1,0:T(8,128)(2,1)S(1)}, bf16[6,128,512]{2,1,0:T(8,128)(2,1)S(1)}, u32[]{:S(2)}, u32[]{:S(2)}) collective-permute-start(bf16[6,128,512]{2,1,0:T(8,128)(2,1)S(1)} %get-tuple-element.10), channel_id=1, source_target_pairs={{0,8},{8,16},{16,24},{24,0},{1,9},{9,17},{17,25},{25,1},{2,10},{10... | collective-permute-start | bytes 2359304 | tf_op jit(solution)/shard_map/ppermute | solution.py:19
  22.2 49.3 %collective-permute-start.8 = (bf16[6,128,512]{2,1,0:T(8,128)(2,1)S(1)}, bf16[6,128,512]{2,1,0:T(8,128)(2,1)S(1)}, u32[]{:S(2)}, u32[]{:S(2)}) collective-permute-start(bf16[6,128,512]{2,1,0:T(8,128)(2,1)S(1)} %get-tuple-element.9), channel_id=1, source_target_pairs={{0,24},{8,0},{16,8},{24,16},{1,25},{9,1},{17,9},{25,17},{2,26},{10... | collective-permute-start | bytes 2359304 | tf_op jit(solution)/shard_map/ppermute | solution.py:19
  22.4 46.0 %collective-permute-start.4 = (bf16[4,128,512]{2,1,0:T(8,128)(2,1)}, bf16[4,128,512]{2,1,0:T(8,128)(2,1)S(1)}, u32[]{:S(2)}, u32[]{:S(2)}) collective-permute-start(bf16[4,128,512]{2,1,0:T(8,128)(2,1)} %get-tuple-element.13), channel_id=1, source_target_pairs={{0,6},{2,0},{4,2},{6,4},{1,7},{3,1},{5,3},{7,5},{8,14},{10,8},{12,... | collective-permute-start | bytes 1572872 | tf_op jit(solution)/shard_map/ppermute | solution.py:19
  23.7 47.8 %collective-permute-start.9 = (bf16[2,128,512]{2,1,0:T(8,128)(2,1)S(1)}, bf16[2,128,512]{2,1,0:T(8,128)(2,1)S(1)}, u32[]{:S(2)}, u32[]{:S(2)}) collective-permute-start(bf16[2,128,512]{2,1,0:T(8,128)(2,1)S(1)} %pad_maximum_fusion.1), channel_id=1, source_target_pairs={{0,2},{2,4},{4,6},{6,0},{1,3},{3,5},{5,7},{7,1},{8,10},{10,12},{12... | collective-permute-start | bytes 786440 | tf_op jit(solution)/shard_map/ppermute | solution.py:19
  24.1 47.4 %collective-permute-start.10 = (bf16[2,128,512]{2,1,0:T(8,128)(2,1)S(1)}, bf16[2,128,512]{2,1,0:T(8,128)(2,1)S(1)}, u32[]{:S(2)}, u32[]{:S(2)}) collective-permute-start(bf16[2,128,512]{2,1,0:T(8,128)(2,1)S(1)} %pad_maximum_fusion.2), channel_id=1, source_target_pairs={{0,6},{2,0},{4,2},{6,4},{1,7},{3,1},{5,3},{7,5},{8,14},{10,8},{12,... | collective-permute-start | bytes 786440 | tf_op jit(solution)/shard_map/ppermute | solution.py:19
  26.2 1.9 %copy-start.2 = (bf16[1,1,64,3,64,128]{5,4,3,2,1,0:T(8,128)(2,1)S(1)}, bf16[1,1,64,3,64,128]{5,4,3,2,1,0:T(8,128)(2,1)}, u32[]{:S(2)}) copy-start(bf16[1,1,64,3,64,128]{5,4,3,2,1,0:T(8,128)(2,1)} %param.17) | copy-start | bytes 9437188

commit v2 on v0

v2 whole, which is shorter than its diff:
```python
import functools

import jax
import jax.numpy as jnp
from jax import lax
from jax.experimental import pallas as pl
from jax.experimental.pallas import tpu as pltpu
from jax.sharding import PartitionSpec as P

ATOMS = 8
GROUP = 4
SMEM = pl.BlockSpec(memory_space=pltpu.SMEM)
VMEM = pl.BlockSpec(memory_space=pltpu.VMEM)


def shift(cells, axis, step):
    count = lax.axis_size(axis)
    return lax.ppermute(cells, axis, [(i, (i + step) % count) for i in range(count)])


def pair_terms(pairs, occ, energy):
    products = []
    for left, right, _, _ in pairs:
        scaled = right.astype(jnp.float32) * occ
        weights = jnp.concatenate(
            (scaled.astype(jnp.bfloat16), (scaled * energy).astype(jnp.bfloat16)), axis=0
        )
        products.append(
            lax.dot_general(
                left, weights, (((1,), (1,)), ((), ())), preferred_element_type=jnp.float32
            )
        )
    parts = []
    for both, (_, right, grad, atoms) in zip(products, pairs):
        basis = right.shape[0]
        density, weighted = both[:, :basis], both[:, basis:]
        terms = jnp.concatenate(
            [
                density * grad(0, c).astype(jnp.float32)
                - weighted * grad(1, c).astype(jnp.float32)
                for c in range(3)
            ],
            axis=1,
        )
        high = terms.astype(jnp.bfloat16)
        low = (terms - high.astype(jnp.float32)).astype(jnp.bfloat16)
        pick = (lax.broadcasted_iota(jnp.int32, (ATOMS, basis), 0) == atoms).astype(jnp.bfloat16)
        parts.append(
            lax.dot_general(
                jnp.concatenate((pick, pick), axis=1),
                jnp.concatenate((high, low), axis=0),
                (((1,), (0,)), ((), ())),
                preferred_element_type=jnp.float32,
            )
        )
    return parts


def sort_kernel(dims, second, meta, lists):
    width_x, width_y, slots = dims
    for k in range(3):
        lists[6 * slots + k] = 0

    def place(s, carry):
        g = second[s]
        gx, gy = g // (width_y + 2) - 1, g % (width_y + 2) - 1
        inside_x = jnp.logical_and(gx >= 0, gx < width_x)
        inside_y = jnp.logical_and(gy >= 0, gy < width_y)
        middle = jnp.logical_and(gy >= 1, gy < width_y - 1)
        row = (gx > 0).astype(jnp.int32)
        column = (gy > 0).astype(jnp.int32)
        stage = jnp.where(
            inside_x, jnp.where(inside_y, 0, 1), jnp.where(middle, 2, 1)
        )
        spot = jnp.where(
            inside_x,
            jnp.where(inside_y, gx * width_y + gy, column * width_x + gx),
            jnp.where(
                middle,
                row * (width_y - 2) + gy - 1,
                2 * width_x + jnp.where(inside_y, 2 * row + column, 4 + 2 * column + row),
            ),
        )
        used = lists[6 * slots + stage]
        lists[stage * slots + used] = s
        lists[(3 + stage) * slots + used] = spot
        lists[6 * slots + stage] = used + 1
        return carry

    lax.fori_loop(0, meta[0], place, 0)


def stage_body(dims, stage, right, first, half, lists, coeffs, grads, occ, energy, atoms, acc):
    slots = dims[2]
    half_rows = grads[0].shape[2]
    number = lists[6 * slots + stage]
    offsets = [pl.multiple_of(part * half_rows, half_rows) for part in (half, 1 - half)]

    def visit(i, carry):
        pairs, targets = [], []
        for q in range(GROUP):
            entry = i * GROUP + q
            place = jnp.minimum(entry, number - 1)
            s = lists[stage * slots + place]
            own = first[s]
            left = jnp.concatenate(
                [coeffs[own, pl.ds(offset, half_rows), :] for offset in offsets], axis=0
            )

            def grad(kind, c, s=s):
                return jnp.concatenate(
                    (grads[2 * kind][s, c], grads[2 * kind + 1][s, c]), axis=0
                )

            pairs.append(
                (
                    left,
                    right(lists[(3 + stage) * slots + place]),
                    grad,
                    atoms[pl.ds(own, 1), :],
                )
            )
            targets.append((own, entry < number))
        for (own, live), part in zip(targets, pair_terms(pairs, occ[...], energy[...])):
            acc[own] += jnp.where(live, part, 0.0)
        return carry

    lax.fori_loop(0, (number + GROUP - 1) // GROUP, visit, 0)


def own_kernel(dims, first, meta, lists, coeffs, gh, gh2, gs, gs2, occ, energy, atoms, acc):
    acc[...] = jnp.zeros_like(acc)
    stage_body(
        dims, 0, lambda spot: coeffs[spot], first, meta[1], lists, coeffs, (gh, gh2, gs, gs2), occ,
        energy, atoms, acc,
    )


def side_kernel(
    dims, first, meta, lists, coeffs, gh, gh2, gs, gs2, occ, energy, atoms, before, *rest
):
    rims, acc, cells, sems = rest[:-3], rest[-3], rest[-2], rest[-1]
    copies, start = [], 0
    for k, rim in enumerate(rims):
        size = rim.shape[0]
        copies.append(pltpu.make_async_copy(rim, cells.at[pl.ds(start, size)], sems.at[k]))
        start += size
    for copy in copies:
        copy.start()
    acc[...] = before[...]
    for copy in copies:
        copy.wait()
    stage_body(
        dims, 1, lambda spot: cells[spot], first, meta[1], lists, coeffs, (gh, gh2, gs, gs2), occ,
        energy, atoms, acc,
    )


def last_kernel(
    dims, first, meta, lists, coeffs, gh, gh2, gs, gs2, occ, energy, atoms, before, low, high, out,
    acc,
):
    acc[...] = before[...]
    width = low.shape[0]

    def right(spot):
        up = spot >= width
        return jnp.where(
            up, high[jnp.maximum(spot - width, 0)], low[jnp.minimum(spot, width - 1)]
        )

    stage_body(
        dims, 2, right, first, meta[1], lists, coeffs, (gh, gh2, gs, gs2), occ, energy, atoms, acc
    )
    basis = atoms.shape[1]
    for c in range(3):
        out[c] = -2.0 * jnp.sum(acc[:, :, c * basis : (c + 1) * basis], axis=2)


def per_device(
    coeffs, occupation, energies, row_atom, pair_first, pair_second, pair_count, deriv_h, deriv_s
):
    width_x, width_y, basis, columns = coeffs.shape
    half_rows = row_atom.shape[2]
    local = width_x * width_y
    slots = pair_first.shape[2]
    dims = (width_x, width_y, slots)

    edge_pair = jnp.stack((coeffs[:, 0], coeffs[:, width_y - 1]), axis=1)
    low_edge = shift(edge_pair[width_x - 1], "cx", 1)
    high_edge = shift(edge_pair[0], "cx", -1)
    low_mid = shift(coeffs[width_x - 1, 1 : width_y - 1], "cx", 1)
    high_mid = shift(coeffs[0, 1 : width_y - 1], "cx", -1)
    low_side = shift(edge_pair[:, 1], "cy", 1)
    high_side = shift(edge_pair[:, 0], "cy", -1)
    low_corner = shift(jnp.stack((low_edge[1], high_edge[1])), "cy", 1)
    high_corner = shift(jnp.stack((low_edge[0], high_edge[0])), "cy", -1)

    grad_h = deriv_h.reshape(slots, 3, half_rows, basis)
    grad_s = deriv_s.reshape(slots, 3, half_rows, basis)
    grads = (grad_h, shift(grad_h, "orb", 1), grad_s, shift(grad_s, "orb", 1))
    atoms_own = row_atom.reshape(local, half_rows)
    atoms = jnp.concatenate((atoms_own, shift(atoms_own, "orb", 1)), axis=1)

    flat = coeffs.reshape(local, basis, columns)
    first, second = pair_first.reshape(slots), pair_second.reshape(slots)
    meta = jnp.stack((pair_count.reshape(()), lax.axis_index("orb").astype(jnp.int32)))
    occ, energy = occupation.reshape(1, columns), energies.reshape(1, columns)

    acc_shape = jax.ShapeDtypeStruct((local, ATOMS, 3 * basis), jnp.float32)
    params = pltpu.CompilerParams(vmem_limit_bytes=16 * 1024 * 1024)

    def cost(share):
        pairs = int(slots * share)
        return pl.CostEstimate(
            flops=pairs * basis * 2 * basis * columns * 2,
            bytes_accessed=pairs * 2 * (2 * basis * columns + 6 * basis * basis),
            transcendentals=0,
        )

    lists = pl.pallas_call(
        functools.partial(sort_kernel, dims),
        out_shape=jax.ShapeDtypeStruct((6 * slots + 8,), jnp.int32),
        in_specs=[SMEM] * 2,
        out_specs=SMEM,
    )(second, meta)
    common = (first, meta, lists, flat, *grads, occ, energy, atoms)
    common_specs = [SMEM] * 3 + [VMEM] * 8
    acc = pl.pallas_call(
        functools.partial(own_kernel, dims),
        out_shape=acc_shape,
        in_specs=common_specs,
        out_specs=VMEM,
        compiler_params=params,
        cost_estimate=cost(0.75),
    )(*common)
    rims = (low_side, high_side, low_edge, high_edge, low_corner, high_corner)
    acc = pl.pallas_call(
        functools.partial(side_kernel, dims),
        out_shape=acc_shape,
        in_specs=common_specs + [VMEM] * (1 + len(rims)),
        out_specs=VMEM,
        scratch_shapes=[
            pltpu.VMEM((sum(rim.shape[0] for rim in rims), basis, columns), jnp.bfloat16),
            pltpu.SemaphoreType.DMA((len(rims),)),
        ],
        compiler_params=params,
        cost_estimate=cost(0.15),
    )(*common, acc, *rims)
    out = pl.pallas_call(
        functools.partial(last_kernel, dims),
        out_shape=jax.ShapeDtypeStruct((3, local, ATOMS), jnp.float32),
        in_specs=common_specs + [VMEM] * 3,
        out_specs=VMEM,
        scratch_shapes=[pltpu.VMEM(acc_shape.shape, jnp.float32)],
        compiler_params=params,
        cost_estimate=cost(0.1),
    )(*common, acc, low_mid, high_mid)
    return lax.psum(out, "orb").reshape(3, width_x, width_y, ATOMS)


def solution(mesh):
    return jax.shard_map(
        per_device,
        mesh=mesh,
        in_specs=(
            P("cx", "cy", None, "orb"),
            P("orb"),
            P("orb"),
            P("cx", "cy", "orb"),
            P("cx", "cy", None),
            P("cx", "cy", None),
            P("cx", "cy"),
            P("cx", "cy", None, None, "orb", None),
            P("cx", "cy", None, None, "orb", None),
        ),
        out_specs=P(None, "cx", "cy", None),
        check_vma=False,
    )
```

time: 468 us -> 72.3 us (0.15)
  the two profiles are of different devices: /device:TPU:15 before, /device:TPU:9 now
where the time goes in v2:
time: 72.3 us; the launch traced here: 71.8 us
  waiting for transfers between devices  23.4 us (32%)
  local copies, waits for them, and re-layouts  16.1 us (22%)
  Pallas kernels  13.9 us (19%)
  starting transfers between devices  9.21 us (13%)
  blocking collectives  6.08 us (8%)
  other arithmetic  2.37 us (3%)
  between operations  0.78 us (1%)
    ppermute x11, waiting for transfers between devices, shift(): lax.ppermute(cells, axis, [(i, (i + step) % count) for i in range(count)])  23.4 us
    unnamed x30, local copies, waits for them, and re-layouts  10.3 us
    ppermute x11, starting transfers between devices, shift(): lax.ppermute(cells, axis, [(i, (i + step) % count) for i in range(count)])  9.21 us
    psum x1, blocking collectives, per_device(): return lax.psum(out, 'orb').reshape(3, width_x, width_y, ATOMS)  6.08 us
    pallas_call x1, Pallas kernels, per_device(): pl.pallas_call(functools.partial(own_kernel, dims), out_shape=acc_shape,...  4.87 us
    pallas_call x1, Pallas kernels, per_device(): pl.pallas_call(functools.partial(last_kernel, dims), out_shape=jax.ShapeD...  3.99 us
    pallas_call x1, Pallas kernels, per_device(): pl.pallas_call(functools.partial(side_kernel, dims), out_shape=acc_shape,...  3.16 us
    squeeze x1, local copies, waits for them, and re-layouts, per_device(): high_mid = shift(coeffs[0, 1:width_y - 1], 'cx', -1)  2.73 us
  transfers between devices with their start and end apart: 11, of which 4 were waited for; matrix products, arithmetic and copies ran while one was open for 11% of the time, Pallas kernels for 14%

profile of v2, /device:TPU:9, one launch (start us, length us, event | category | flops | bytes accessed | tf_op | source)
XLA Modules:
  0.0 71.8 jit_solution(15630018737406270525)
XLA Ops:
  0.7 2.3 %fusion.1 = (bf16[4,1,128,512]{3,2,1,0:T(8,128)(2,1)S(1)}, bf16[4,128,512]{2,1,0:T(8,128)(2,1)}, bf16[4,128,512]{2,1,0:T(8,128)(2,1)}, bf16[4,1,128,512]{3,2,1,0:T(8,128)(2,1)S(1)}) fusion(bf16[4,8,128,512]{3,2,1,0:T(8,128)(2,1)} %param.9), kind=kLoop, calls=%fused_computation.11 | loop fusion | bytes 3145728 | tf_op jit(solution)/shard_map/slice | solution.py:189
  3.2 1.3 %collective-permute-start.5 = (bf16[2,128,512]{2,1,0:T(8,128)(2,1)S(1)}, bf16[2,128,512]{2,1,0:T(8,128)(2,1)S(1)}, u32[]{:S(2)}, u32[]{:S(2)}) collective-permute-start(bf16[2,128,512]{2,1,0:T(8,128)(2,1)S(1)} %get-tuple-element.12), channel_id=1, source_target_pairs={{0,8},{8,16},{16,24},{24,0},{1,9},{9,17},{17,25},{25,1},{2,10},{10... | collective-permute-start | bytes 786440 | tf_op jit(solution)/shard_map/ppermute | solution.py:18
  4.7 1.0 %collective-permute-start.2 = (s32[32,64]{1,0:T(8,128)S(1)}, s32[32,64]{1,0:T(8,128)}, u32[]{:S(2)}, u32[]{:S(2)}) collective-permute-start(s32[32,64]{1,0:T(8,128)S(1)} %bitcast.46), channel_id=1, source_target_pairs={{0,1},{1,0},{2,3},{3,2},{4,5},{5,4},{6,7},{7,6},{8,9},{9,8},{10,11... | collective-permute-start | bytes 24584 | tf_op jit(solution)/shard_map/ppermute | solution.py:18
  5.7 5.0 %collective-permute-done.5.rest_2_ = bf16[2,128,512]{2,1,0:T(8,128)(2,1)S(1)} collective-permute-done((bf16[2,128,512]{2,1,0:T(8,128)(2,1)S(1)}, bf16[2,128,512]{2,1,0:T(8,128)(2,1)S(1)}, u32[]{:S(2)}, u32[]{:S(2)}) %collective-permute-start.5) | collective-permute-done | bytes 262176 | tf_op jit(solution)/shard_map/ppermute | solution.py:18
  10.7 7.2 %collective-permute-done.6.rest_3_ = bf16[2,128,512]{2,1,0:T(8,128)(2,1)S(1)} collective-permute-done((bf16[2,128,512]{2,1,0:T(8,128)(2,1)S(1)}, bf16[2,128,512]{2,1,0:T(8,128)(2,1)S(1)}, u32[]{:S(2)}, u32[]{:S(2)}) %collective-permute-start.6) | collective-permute-done | bytes 262176 | tf_op jit(solution)/shard_map/ppermute | solution.py:18
  19.3 1.3 %collective-permute-start.7 = (bf16[2,128,512]{2,1,0:T(8,128)(2,1)S(1)}, bf16[2,128,512]{2,1,0:T(8,128)(2,1)S(1)}, u32[]{:S(2)}, u32[]{:S(2)}) collective-permute-start(bf16[2,128,512]{2,1,0:T(8,128)(2,1)S(1)} %pad_maximum_fusion.1), channel_id=1, source_target_pairs={{0,2},{2,4},{4,6},{6,0},{1,3},{3,5},{5,7},{7,1},{8,10},{10,12},{12... | collective-permute-start | bytes 786440 | tf_op jit(solution)/shard_map/ppermute | solution.py:18
  20.6 2.7 %slice_bitcast_fusion = (bf16[6,128,512]{2,1,0:T(8,128)(2,1)}, bf16[6,128,512]{2,1,0:T(8,128)(2,1)}) fusion(bf16[4,8,128,512]{3,2,1,0:T(8,128)(2,1)} %param.9), kind=kLoop, calls=%fused_computation | loop fusion | bytes 3145728 | tf_op jit(solution)/shard_map/squeeze | solution.py:193
  23.3 1.4 %collective-permute-start.9 = (bf16[6,128,512]{2,1,0:T(8,128)(2,1)}, bf16[6,128,512]{2,1,0:T(8,128)(2,1)}, u32[]{:S(2)}, u32[]{:S(2)}) collective-permute-start(bf16[6,128,512]{2,1,0:T(8,128)(2,1)} %get-tuple-element.6), channel_id=1, source_target_pairs={{0,8},{8,16},{16,24},{24,0},{1,9},{9,17},{17,25},{25,1},{2,10},{10... | collective-permute-start | bytes 2359304 | tf_op jit(solution)/shard_map/ppermute | solution.py:18
  24.8 2.9 %collective-permute-done.7.rest_4_ = bf16[2,128,512]{2,1,0:T(8,128)(2,1)S(1)} collective-permute-done((bf16[2,128,512]{2,1,0:T(8,128)(2,1)S(1)}, bf16[2,128,512]{2,1,0:T(8,128)(2,1)S(1)}, u32[]{:S(2)}, u32[]{:S(2)}) %collective-permute-start.7) | collective-permute-done | bytes 262176 | tf_op jit(solution)/shard_map/ppermute | solution.py:18
  27.6 0.7 copy-done.7
  28.7 1.7 %copy-done.3 = bf16[64,3,64,128]{3,2,1,0:T(8,128)(2,1)} copy-done((bf16[64,3,64,128]{3,2,1,0:T(8,128)(2,1)}, bf16[64,3,64,128]{3,2,1,0:T(8,128)(2,1)S(1)}, u32[]{:S(2)}) %copy-start.3) | copy-done | bytes 3145752
  30.3 2.1 %collective-permute-start.4 = (bf16[4,128,512]{2,1,0:T(8,128)(2,1)}, bf16[4,128,512]{2,1,0:T(8,128)(2,1)}, u32[]{:S(2)}, u32[]{:S(2)}) collective-permute-start(bf16[4,128,512]{2,1,0:T(8,128)(2,1)} %get-tuple-element.9), channel_id=1, source_target_pairs={{0,6},{2,0},{4,2},{6,4},{1,7},{3,1},{5,3},{7,5},{8,14},{10,8},{12,... | collective-permute-start | bytes 1572872 | tf_op jit(solution)/shard_map/ppermute | solution.py:18
  33.6 1.9 %shard_map.91.lists = s32[392]{0:T(512)} custom-call(s32[64]{0:T(128)} %bitcast.47, s32[2]{0:T(128)} %pad_add_fusion.1.meta), custom_call_target="tpu_custom_call" | custom-call | tf_op jit(solution)/shard_map/pallas_call | solution.py:221
  35.5 0.9 %pad_maximum_fusion.2 = bf16[2,128,512]{2,1,0:T(8,128)(2,1)S(1)} fusion(bf16[1,128,512]{2,1,0:T(8,128)(2,1)} %get-tuple-element.15, bf16[1,128,512]{2,1,0:T(8,128)(2,1)S(1)} %get-tuple-element.13), kind=kLoop, calls=%fused_computation.6 | loop fusion | flops 131072 | bytes 524288 | tf_op jit(solution)/shard_map/stack | solution.py:197
  36.4 0.9 %collective-permute-start.8 = (bf16[2,128,512]{2,1,0:T(8,128)(2,1)S(1)}, bf16[2,128,512]{2,1,0:T(8,128)(2,1)S(1)}, u32[]{:S(2)}, u32[]{:S(2)}) collective-permute-start(bf16[2,128,512]{2,1,0:T(8,128)(2,1)S(1)} %pad_maximum_fusion.2), channel_id=1, source_target_pairs={{0,6},{2,0},{4,2},{6,4},{1,7},{3,1},{5,3},{7,5},{8,14},{10,8},{12,... | collective-permute-start | bytes 786440 | tf_op jit(solution)/shard_map/ppermute | solution.py:18
  37.3 0.8 %pad_add_fusion.atoms = s32[32,128]{1,0:T(8,128)S(1)} fusion(s32[32,64]{1,0:T(8,128)} %collective-permute-done.2, s32[32,64]{1,0:T(8,128)} %bitcast.45), kind=kLoop, calls=%fused_computation.7 | loop fusion | flops 4096 | bytes 32768 | tf_op jit(solution)/shard_map/concatenate | solution.py:203
  38.1 2.2 %copy-done = bf16[4,8,128,512]{3,2,1,0:T(8,128)(2,1)S(1)} copy-done((bf16[4,8,128,512]{3,2,1,0:T(8,128)(2,1)S(1)}, bf16[4,8,128,512]{3,2,1,0:T(8,128)(2,1)}, u32[]{:S(2)}) %copy-start) | copy-done | bytes 4194328
  40.3 1.9 %copy-done.2 = bf16[1,1,64,3,64,128]{5,4,3,2,1,0:T(8,128)(2,1)S(1)} copy-done((bf16[1,1,64,3,64,128]{5,4,3,2,1,0:T(8,128)(2,1)S(1)}, bf16[1,1,64,3,64,128]{5,4,3,2,1,0:T(8,128)(2,1)}, u32[]{:S(2)}) %copy-start.2) | copy-done | bytes 3145752
  42.2 1.9 %copy-done.4 = bf16[64,3,64,128]{3,2,1,0:T(8,128)(2,1)S(1)} copy-done((bf16[64,3,64,128]{3,2,1,0:T(8,128)(2,1)S(1)}, bf16[64,3,64,128]{3,2,1,0:T(8,128)(2,1)}, u32[]{:S(2)}) %copy-start.4) | copy-done | bytes 3145752
  45.4 4.9 %shard_map.92.before = f32[32,8,384]{2,1,0:T(8,128)S(1)} custom-call(s32[64]{0:T(128)S(1)} %bitcast.42, s32[2]{0:T(128)S(1)} %copy-done.12, s32[392]{0:T(512)S(1)} %copy-done.9, bf16[32,128,512]{2,1,0:T(8,128)(2,1)S(1)} %bitcast.24, bf16[64,3,64,128]{3,2,1,0:T(8,128)(2,1)S(1)} %bitcast.28, bf16[64,3,64,128]{3,2,1,0:T(8,128)(2,1)S(1)} %copy-done.4, ...), custom_call_target="tpu_custom_call" | custom-call | flops 1610612736 | bytes 22020096 | tf_op jit(solution)/shard_map/pallas_call | solution.py:229
  50.2 8.3 %collective-permute-done.8.rest_5_ = bf16[2,128,512]{2,1,0:T(8,128)(2,1)S(1)} collective-permute-done((bf16[2,128,512]{2,1,0:T(8,128)(2,1)S(1)}, bf16[2,128,512]{2,1,0:T(8,128)(2,1)S(1)}, u32[]{:S(2)}, u32[]{:S(2)}) %collective-permute-start.8) | collective-permute-done | bytes 262176 | tf_op jit(solution)/shard_map/ppermute | solution.py:18
  58.6 3.2 %shard_map.93.before = f32[32,8,384]{2,1,0:T(8,128)S(1)} custom-call(s32[64]{0:T(128)S(1)} %bitcast.43, s32[2]{0:T(128)S(1)} %copy-done.12, s32[392]{0:T(512)S(1)} %copy-done.9, bf16[32,128,512]{2,1,0:T(8,128)(2,1)S(1)} %bitcast.25, bf16[64,3,64,128]{3,2,1,0:T(8,128)(2,1)S(1)} %bitcast.29, bf16[64,3,64,128]{3,2,1,0:T(8,128)(2,1)S(1)} %copy-done.4, ...), custom_call_target="tpu_custom_call" | custom-call | flops 301989888 | bytes 4128768 | tf_op jit(solution)/shard_map/pallas_call | solution.py:238
  61.8 4.0 %shard_map.94 = f32[3,32,8]{2,1,0:T(8,128)S(1)} custom-call(s32[64]{0:T(128)S(1)} %bitcast.44, s32[2]{0:T(128)S(1)} %copy-done.12, s32[392]{0:T(512)S(1)} %copy-done.9, bf16[32,128,512]{2,1,0:T(8,128)(2,1)S(1)} %bitcast.26, bf16[64,3,64,128]{3,2,1,0:T(8,128)(2,1)S(1)} %bitcast.30, bf16[64,3,64,128]{3,2,1,0:T(8,128)(2,1)S(1)} %copy-done.4, ...), custom_call_target="tpu_custom_call" | custom-call | flops 201326592 | bytes 2752512 | tf_op jit(solution)/shard_map/pallas_call | solution.py:250
  65.7 6.1 %psum.7 = f32[3,4,8,8]{3,2,1,0:T(8,128)} all-reduce(f32[3,4,8,8]{3,2,1,0:T(8,128)S(1)} %bitcast.35), channel_id=1, replica_groups=mesh['cx'=4,'cy'=4,'orb'=2] {'orb'}, use_global_device_ids=true, to_apply=%region_0.0 | all-reduce | flops 768 | bytes 6144 | tf_op jit(solution)/shard_map/psum | solution.py:259
  (42 shorter events, 4.6 us)
Async XLA Ops:
  0.0 4.7 %copy-start.14 = (s32[4,8,64]{2,1,0:T(8,128)S(1)}, s32[4,8,64]{2,1,0:T(8,128)}, u32[]{:S(2)}) copy-start(s32[4,8,64]{2,1,0:T(8,128)} %param.12) | copy-start | bytes 24580
  0.0 28.7 %collective-permute-start = (bf16[64,3,64,128]{3,2,1,0:T(8,128)(2,1)}, bf16[64,3,64,128]{3,2,1,0:T(8,128)(2,1)S(1)}, u32[]{:S(2)}, u32[]{:S(2)}) collective-permute-start(bf16[64,3,64,128]{3,2,1,0:T(8,128)(2,1)} %bitcast.27), channel_id=1, source_target_pairs={{0,1},{1,0},{2,3},{3,2},{4,5},{5,4},{6,7},{7,6},{8,9},{9,8},{10,11... | collective-permute-start | bytes 9437192 | tf_op jit(solution)/shard_map/ppermute | solution.py:18
  0.7 35.8 %collective-permute-start.1 = (bf16[64,3,64,128]{3,2,1,0:T(8,128)(2,1)}, bf16[64,3,64,128]{3,2,1,0:T(8,128)(2,1)}, u32[]{:S(2)}, u32[]{:S(2)}) collective-permute-start(bf16[64,3,64,128]{3,2,1,0:T(8,128)(2,1)} %bitcast.31), channel_id=1, source_target_pairs={{0,1},{1,0},{2,3},{3,2},{4,5},{5,4},{6,7},{7,6},{8,9},{9,8},{10,11... | collective-permute-start | bytes 9437192 | tf_op jit(solution)/shard_map/ppermute | solution.py:18
  3.1 35.0 %copy-start.1 = (bf16[1,1,64,3,64,128]{5,4,3,2,1,0:T(8,128)(2,1)S(1)}, bf16[1,1,64,3,64,128]{5,4,3,2,1,0:T(8,128)(2,1)}, u32[]{:S(2)}) copy-start(bf16[1,1,64,3,64,128]{5,4,3,2,1,0:T(8,128)(2,1)} %param.16) | copy-start | bytes 9437188
  3.1 35.0 %copy-start.10 = (f32[512]{0:T(512)S(1)}, f32[512]{0:T(512)}, u32[]{:S(2)}) copy-start(f32[512]{0:T(512)} %param.10) | copy-start | bytes 6148
  3.1 35.0 %copy-start.11 = (f32[512]{0:T(512)S(1)}, f32[512]{0:T(512)}, u32[]{:S(2)}) copy-start(f32[512]{0:T(512)} %param.11) | copy-start | bytes 6148
  3.1 35.0 %copy-start.13 = (s32[1,1,64]{2,1,0:T(1,128)S(1)}, s32[1,1,64]{2,1,0:T(1,128)}, u32[]{:S(2)}) copy-start(s32[1,1,64]{2,1,0:T(1,128)} %param.13) | copy-start | bytes 772
  3.2 7.5 %collective-permute-start.5 = (bf16[2,128,512]{2,1,0:T(8,128)(2,1)S(1)}, bf16[2,128,512]{2,1,0:T(8,128)(2,1)S(1)}, u32[]{:S(2)}, u32[]{:S(2)}) collective-permute-start(bf16[2,128,512]{2,1,0:T(8,128)(2,1)S(1)} %get-tuple-element.12), channel_id=1, source_target_pairs={{0,8},{8,16},{16,24},{24,0},{1,9},{9,17},{17,25},{25,1},{2,10},{10... | collective-permute-start | bytes 786440 | tf_op jit(solution)/shard_map/ppermute | solution.py:18
  4.5 13.4 %collective-permute-start.6 = (bf16[2,128,512]{2,1,0:T(8,128)(2,1)S(1)}, bf16[2,128,512]{2,1,0:T(8,128)(2,1)S(1)}, u32[]{:S(2)}, u32[]{:S(2)}) collective-permute-start(bf16[2,128,512]{2,1,0:T(8,128)(2,1)S(1)} %get-tuple-element.11), channel_id=1, source_target_pairs={{0,24},{8,0},{16,8},{24,16},{1,25},{9,1},{17,9},{25,17},{2,26},{10... | collective-permute-start | bytes 786440 | tf_op jit(solution)/shard_map/ppermute | solution.py:18
  4.7 18.6 %collective-permute-start.2 = (s32[32,64]{1,0:T(8,128)S(1)}, s32[32,64]{1,0:T(8,128)}, u32[]{:S(2)}, u32[]{:S(2)}) collective-permute-start(s32[32,64]{1,0:T(8,128)S(1)} %bitcast.46), channel_id=1, source_target_pairs={{0,1},{1,0},{2,3},{3,2},{4,5},{5,4},{6,7},{7,6},{8,9},{9,8},{10,11... | collective-permute-start | bytes 24584 | tf_op jit(solution)/shard_map/ppermute | solution.py:18
  18.6 0.7 copy-start.5
  19.3 8.3 %collective-permute-start.7 = (bf16[2,128,512]{2,1,0:T(8,128)(2,1)S(1)}, bf16[2,128,512]{2,1,0:T(8,128)(2,1)S(1)}, u32[]{:S(2)}, u32[]{:S(2)}) collective-permute-start(bf16[2,128,512]{2,1,0:T(8,128)(2,1)S(1)} %pad_maximum_fusion.1), channel_id=1, source_target_pairs={{0,2},{2,4},{4,6},{6,0},{1,3},{3,5},{5,7},{7,1},{8,10},{10,12},{12... | collective-permute-start | bytes 786440 | tf_op jit(solution)/shard_map/ppermute | solution.py:18
  23.3 38.5 %collective-permute-start.10 = (bf16[6,128,512]{2,1,0:T(8,128)(2,1)}, bf16[6,128,512]{2,1,0:T(8,128)(2,1)}, u32[]{:S(2)}, u32[]{:S(2)}) collective-permute-start(bf16[6,128,512]{2,1,0:T(8,128)(2,1)} %get-tuple-element.5), channel_id=1, source_target_pairs={{0,24},{8,0},{16,8},{24,16},{1,25},{9,1},{17,9},{25,17},{2,26},{10... | collective-permute-start | bytes 2359304 | tf_op jit(solution)/shard_map/ppermute | solution.py:18
  23.3 38.4 %collective-permute-start.9 = (bf16[6,128,512]{2,1,0:T(8,128)(2,1)}, bf16[6,128,512]{2,1,0:T(8,128)(2,1)}, u32[]{:S(2)}, u32[]{:S(2)}) collective-permute-start(bf16[6,128,512]{2,1,0:T(8,128)(2,1)} %get-tuple-element.6), channel_id=1, source_target_pairs={{0,8},{8,16},{16,24},{24,0},{1,9},{9,17},{17,25},{25,1},{2,10},{10... | collective-permute-start | bytes 2359304 | tf_op jit(solution)/shard_map/ppermute | solution.py:18
  27.6 0.7 copy-start.7
  28.3 30.2 %collective-permute-start.3 = (bf16[4,128,512]{2,1,0:T(8,128)(2,1)}, bf16[4,128,512]{2,1,0:T(8,128)(2,1)}, u32[]{:S(2)}, u32[]{:S(2)}) collective-permute-start(bf16[4,128,512]{2,1,0:T(8,128)(2,1)} %get-tuple-element.8), channel_id=1, source_target_pairs={{0,2},{2,4},{4,6},{6,0},{1,3},{3,5},{5,7},{7,1},{8,10},{10,12},{12... | collective-permute-start | bytes 1572872 | tf_op jit(solution)/shard_map/ppermute | solution.py:18
  28.7 1.7 %copy-start.3 = (bf16[64,3,64,128]{3,2,1,0:T(8,128)(2,1)}, bf16[64,3,64,128]{3,2,1,0:T(8,128)(2,1)S(1)}, u32[]{:S(2)}) copy-start(bf16[64,3,64,128]{3,2,1,0:T(8,128)(2,1)S(1)} %collective-permute-done.gh2) | copy-start | bytes 9437188
  30.3 28.2 %collective-permute-start.4 = (bf16[4,128,512]{2,1,0:T(8,128)(2,1)}, bf16[4,128,512]{2,1,0:T(8,128)(2,1)}, u32[]{:S(2)}, u32[]{:S(2)}) collective-permute-start(bf16[4,128,512]{2,1,0:T(8,128)(2,1)} %get-tuple-element.9), channel_id=1, source_target_pairs={{0,6},{2,0},{4,2},{6,4},{1,7},{3,1},{5,3},{7,5},{8,14},{10,8},{12,... | collective-permute-start | bytes 1572872 | tf_op jit(solution)/shard_map/ppermute | solution.py:18
  36.4 22.1 %collective-permute-start.8 = (bf16[2,128,512]{2,1,0:T(8,128)(2,1)S(1)}, bf16[2,128,512]{2,1,0:T(8,128)(2,1)S(1)}, u32[]{:S(2)}, u32[]{:S(2)}) collective-permute-start(bf16[2,128,512]{2,1,0:T(8,128)(2,1)S(1)} %pad_maximum_fusion.2), channel_id=1, source_target_pairs={{0,6},{2,0},{4,2},{6,4},{1,7},{3,1},{5,3},{7,5},{8,14},{10,8},{12,... | collective-permute-start | bytes 786440 | tf_op jit(solution)/shard_map/ppermute | solution.py:18
  38.1 2.2 %copy-start = (bf16[4,8,128,512]{3,2,1,0:T(8,128)(2,1)S(1)}, bf16[4,8,128,512]{3,2,1,0:T(8,128)(2,1)}, u32[]{:S(2)}) copy-start(bf16[4,8,128,512]{3,2,1,0:T(8,128)(2,1)} %param.9) | copy-start | bytes 12582916
  40.3 1.9 %copy-start.2 = (bf16[1,1,64,3,64,128]{5,4,3,2,1,0:T(8,128)(2,1)S(1)}, bf16[1,1,64,3,64,128]{5,4,3,2,1,0:T(8,128)(2,1)}, u32[]{:S(2)}) copy-start(bf16[1,1,64,3,64,128]{5,4,3,2,1,0:T(8,128)(2,1)} %param.17) | copy-start | bytes 9437188
  42.2 1.9 %copy-start.4 = (bf16[64,3,64,128]{3,2,1,0:T(8,128)(2,1)S(1)}, bf16[64,3,64,128]{3,2,1,0:T(8,128)(2,1)}, u32[]{:S(2)}) copy-start(bf16[64,3,64,128]{3,2,1,0:T(8,128)(2,1)} %copy-done.3) | copy-start | bytes 9437188
  45.4 13.2 %copy-start.6 = (bf16[2,128,512]{2,1,0:T(8,128)(2,1)S(1)}, bf16[2,128,512]{2,1,0:T(8,128)(2,1)}, u32[]{:S(2)}) copy-start(bf16[2,128,512]{2,1,0:T(8,128)(2,1)} %copy-done.5) | copy-start | bytes 786436
  45.4 13.2 %copy-start.8 = (bf16[2,128,512]{2,1,0:T(8,128)(2,1)S(1)}, bf16[2,128,512]{2,1,0:T(8,128)(2,1)}, u32[]{:S(2)}) copy-start(bf16[2,128,512]{2,1,0:T(8,128)(2,1)} %copy-done.7) | copy-start | bytes 786436
  (2 other events, 1.3 us)

commit v3 on v2

v3 whole, which is shorter than its diff:
```python
import functools

import jax
import jax.numpy as jnp
from jax import lax
from jax.experimental import pallas as pl
from jax.experimental.pallas import tpu as pltpu
from jax.sharding import PartitionSpec as P

ATOMS = 8
GROUP = 4
CHUNK = 8
ANY = pl.BlockSpec(memory_space=pl.ANY)
SMEM = pl.BlockSpec(memory_space=pltpu.SMEM)
VMEM = pl.BlockSpec(memory_space=pltpu.VMEM)


def shift(cells, axis, step):
    count = lax.axis_size(axis)
    return lax.ppermute(cells, axis, [(i, (i + step) % count) for i in range(count)])


def after(cells, *others):
    return lax.optimization_barrier((cells, *others))[0]


def pair_terms(pairs, occ, energy):
    products = []
    for left, right, _, _ in pairs:
        scaled = right.astype(jnp.float32) * occ
        weights = jnp.concatenate(
            (scaled.astype(jnp.bfloat16), (scaled * energy).astype(jnp.bfloat16)), axis=0
        )
        products.append(
            lax.dot_general(
                left, weights, (((1,), (1,)), ((), ())), preferred_element_type=jnp.float32
            )
        )
    parts = []
    for both, (_, right, grad, atoms) in zip(products, pairs):
        basis = right.shape[0]
        density, weighted = both[:, :basis], both[:, basis:]
        terms = jnp.concatenate(
            [
                density * grad(0, c).astype(jnp.float32)
                - weighted * grad(1, c).astype(jnp.float32)
                for c in range(3)
            ],
            axis=1,
        )
        high = terms.astype(jnp.bfloat16)
        low = (terms - high.astype(jnp.float32)).astype(jnp.bfloat16)
        pick = (lax.broadcasted_iota(jnp.int32, (ATOMS, basis), 0) == atoms).astype(jnp.bfloat16)
        parts.append(
            lax.dot_general(
                jnp.concatenate((pick, pick), axis=1),
                jnp.concatenate((high, low), axis=0),
                (((1,), (0,)), ((), ())),
                preferred_element_type=jnp.float32,
            )
        )
    return parts


def sort_kernel(dims, first, second, meta, table):
    width_x, width_y, slots = dims
    tail = 9 * slots
    for k in range(3):
        table[tail + k] = 0
    table[tail + 3] = meta[1]
    table[tail + 4] = meta[0]

    def place(s, carry):
        g = second[s]
        gx, gy = g // (width_y + 2) - 1, g % (width_y + 2) - 1
        inside_x = jnp.logical_and(gx >= 0, gx < width_x)
        inside_y = jnp.logical_and(gy >= 0, gy < width_y)
        at_end = jnp.logical_or(gy == 0, gy == width_y - 1)
        row = (gx > 0).astype(jnp.int32)
        column = (gy > 0).astype(jnp.int32)
        stage = jnp.where(inside_x, jnp.where(inside_y, 0, 1), jnp.where(at_end, 1, 2))
        spot = jnp.where(
            inside_x,
            jnp.where(inside_y, gx * width_y + gy, column * width_x + gx),
            jnp.where(
                inside_y,
                jnp.where(at_end, 2 * width_x + 2 * row + column, row * (width_y - 2) + gy - 1),
                2 * (width_y - 2) + 2 * column + row,
            ),
        )
        used = table[tail + stage]
        base = stage * 3 * slots + used
        table[base] = s
        table[base + slots] = first[s]
        table[base + 2 * slots] = spot
        table[tail + stage] = used + 1
        return carry

    lax.fori_loop(0, meta[0], place, 0)


def stage_body(
    dims, stage, right, table, coeffs, grads, occ, energy, atoms, acc, ready=lambda slot, done: done
):
    slots = dims[2]
    half_rows = grads[0].shape[2]
    number, half = table[9 * slots + stage], table[9 * slots + 3]
    offsets = [pl.multiple_of(part * half_rows, half_rows) for part in (half, 1 - half)]

    def visit(i, done):
        final = jnp.minimum(i * GROUP + GROUP - 1, number - 1)
        done = ready(table[stage * 3 * slots + final], done)
        pairs, targets = [], []
        for q in range(GROUP):
            entry = i * GROUP + q
            base = stage * 3 * slots + jnp.minimum(entry, number - 1)
            s, own, spot = table[base], table[base + slots], table[base + 2 * slots]
            left = jnp.concatenate(
                [coeffs[own, pl.ds(offset, half_rows), :] for offset in offsets], axis=0
            )

            def grad(kind, c, s=s):
                return jnp.concatenate(
                    (grads[2 * kind][s, c], grads[2 * kind + 1][s, c]), axis=0
                )

            pairs.append((left, right(spot), grad, atoms[pl.ds(own, 1), :]))
            targets.append((own, entry < number))
        for (own, live), part in zip(targets, pair_terms(pairs, occ[...], energy[...])):
            acc[own] += jnp.where(live, part, 0.0)
        return done

    return lax.fori_loop(0, (number + GROUP - 1) // GROUP, visit, 0)


def own_kernel(
    dims, table, coeffs, gh, gs, gh_far, gs_far, occ, energy, atoms, acc, gh2, gs2, sems
):
    slots = dims[2]
    chunks = (table[9 * slots + 4] + CHUNK - 1) // CHUNK

    def copies(k):
        part = pl.ds(pl.multiple_of(k * CHUNK, CHUNK), CHUNK)
        return [
            pltpu.make_async_copy(far.at[part], near.at[part], sems.at[k, n])
            for n, (far, near) in enumerate(((gh_far, gh2), (gs_far, gs2)))
        ]

    def start(k, carry):
        for copy in copies(k):
            copy.start()
        return carry

    def wait(k, carry):
        for copy in copies(k):
            copy.wait()
        return carry

    def ready(slot, done):
        need = jnp.maximum(slot // CHUNK + 1, done)
        lax.fori_loop(done, need, wait, 0)
        return need

    lax.fori_loop(0, chunks, start, 0)
    acc[...] = jnp.zeros_like(acc)
    done = stage_body(
        dims, 0, lambda spot: coeffs[spot], table, coeffs, (gh, gh2, gs, gs2), occ, energy, atoms,
        acc, ready,
    )
    lax.fori_loop(done, chunks, wait, 0)


def side_kernel(
    dims, table, coeffs, gh, gh2, gs, gs2, occ, energy, atoms, before, *rest
):
    rims, acc, cells, sems = rest[:-3], rest[-3], rest[-2], rest[-1]
    copies, start = [], 0
    for k, rim in enumerate(rims):
        size = rim.shape[0]
        copies.append(pltpu.make_async_copy(rim, cells.at[pl.ds(start, size)], sems.at[k]))
        start += size
    for copy in copies:
        copy.start()
    acc[...] = before[...]
    for copy in copies:
        copy.wait()
    stage_body(
        dims, 1, lambda spot: cells[spot], table, coeffs, (gh, gh2, gs, gs2), occ, energy, atoms, acc,
    )


def last_kernel(
    dims, table, coeffs, gh, gh2, gs, gs2, occ, energy, atoms, before, *rest
):
    rims, out, acc = rest[:-2], rest[-2], rest[-1]
    acc[...] = before[...]

    def right(spot):
        start, cell = 0, None
        for rim in rims:
            size = rim.shape[0]
            here = rim[jnp.clip(spot - start, 0, size - 1)]
            cell = here if cell is None else jnp.where(spot >= start, here, cell)
            start += size
        return cell

    stage_body(
        dims, 2, right, table, coeffs, (gh, gh2, gs, gs2), occ, energy, atoms, acc
    )
    basis = atoms.shape[1]
    for c in range(3):
        out[c] = -2.0 * jnp.sum(acc[:, :, c * basis : (c + 1) * basis], axis=2)


def per_device(
    coeffs, occupation, energies, row_atom, pair_first, pair_second, pair_count, deriv_h, deriv_s
):
    width_x, width_y, basis, columns = coeffs.shape
    half_rows = row_atom.shape[2]
    local = width_x * width_y
    slots = pair_first.shape[2]
    dims = (width_x, width_y, slots)

    grad_h = deriv_h.reshape(slots, 3, half_rows, basis)
    grad_s = deriv_s.reshape(slots, 3, half_rows, basis)
    grad_h_far, grad_s_far = shift(grad_h, "orb", 1), shift(grad_s, "orb", 1)
    low_edge = shift(coeffs[width_x - 1, :: width_y - 1], "cx", 1)
    high_edge = shift(coeffs[0, :: width_y - 1], "cx", -1)
    low_mid = shift(coeffs[width_x - 1, 1 : width_y - 1], "cx", 1)
    low_side = shift(after(coeffs[:, width_y - 1], low_edge), "cy", 1)
    high_side = shift(after(coeffs[:, 0], high_edge), "cy", -1)
    high_mid = shift(coeffs[0, 1 : width_y - 1], "cx", -1)
    low_corner = shift(jnp.stack((low_edge[1], high_edge[1])), "cy", 1)
    high_corner = shift(jnp.stack((low_edge[0], high_edge[0])), "cy", -1)

    half = lax.axis_index("orb")
    atoms_own = row_atom.reshape(local, half_rows)
    atoms_all = lax.all_gather(atoms_own, "orb", axis=0)
    atoms = jnp.concatenate(
        (atoms_own, jnp.where(half == 0, atoms_all[1], atoms_all[0])), axis=1
    )

    flat = coeffs.reshape(local, basis, columns)
    first, second = pair_first.reshape(slots), pair_second.reshape(slots)
    meta = jnp.stack((pair_count.reshape(()), half.astype(jnp.int32)))
    occ, energy = occupation.reshape(1, columns), energies.reshape(1, columns)

    acc_shape = jax.ShapeDtypeStruct((local, ATOMS, 3 * basis), jnp.float32)
    params = pltpu.CompilerParams(vmem_limit_bytes=6 * 1024 * 1024)

    def cost(share):
        pairs = int(slots * share)
        return pl.CostEstimate(
            flops=pairs * basis * 2 * basis * columns * 2,
            bytes_accessed=pairs * 2 * (2 * basis * columns + 6 * basis * basis),
            transcendentals=0,
        )

    table = pl.pallas_call(
        functools.partial(sort_kernel, dims),
        out_shape=jax.ShapeDtypeStruct((9 * slots + 8,), jnp.int32),
        in_specs=[SMEM] * 3,
        out_specs=SMEM,
        compiler_params=pltpu.CompilerParams(vmem_limit_bytes=1024 * 1024),
    )(first, second, meta)
    acc, grad_h2, grad_s2 = pl.pallas_call(
        functools.partial(own_kernel, dims),
        out_shape=(
            acc_shape,
            jax.ShapeDtypeStruct(grad_h.shape, grad_h.dtype),
            jax.ShapeDtypeStruct(grad_s.shape, grad_s.dtype),
        ),
        in_specs=[SMEM] + [VMEM] * 3 + [ANY] * 2 + [VMEM] * 3,
        out_specs=(VMEM, VMEM, VMEM),
        scratch_shapes=[pltpu.SemaphoreType.DMA((slots // CHUNK, 2))],
        compiler_params=params,
        cost_estimate=cost(0.75),
    )(table, flat, grad_h, grad_s, grad_h_far, grad_s_far, occ, energy, atoms)
    common = (table, flat, grad_h, grad_h2, grad_s, grad_s2, occ, energy, atoms)
    common_specs = [SMEM] + [VMEM] * 8
    rims = (low_side, high_side, low_edge, high_edge)
    acc = pl.pallas_call(
        functools.partial(side_kernel, dims),
        out_shape=acc_shape,
        in_specs=common_specs + [VMEM] * (1 + len(rims)),
        out_specs=VMEM,
        scratch_shapes=[
            pltpu.VMEM((sum(rim.shape[0] for rim in rims), basis, columns), jnp.bfloat16),
            pltpu.SemaphoreType.DMA((len(rims),)),
        ],
        compiler_params=params,
        cost_estimate=cost(0.15),
    )(*common, acc, *rims)
    out = pl.pallas_call(
        functools.partial(last_kernel, dims),
        out_shape=jax.ShapeDtypeStruct((3, local, ATOMS), jnp.float32),
        in_specs=common_specs + [VMEM] * 5,
        out_specs=VMEM,
        scratch_shapes=[pltpu.VMEM(acc_shape.shape, jnp.float32)],
        compiler_params=params,
        cost_estimate=cost(0.1),
    )(*common, acc, low_mid, high_mid, low_corner, high_corner)
    total = out + shift(out, "orb", 1)
    return total.reshape(3, width_x, width_y, ATOMS)


def solution(mesh):
    return jax.shard_map(
        per_device,
        mesh=mesh,
        in_specs=(
            P("cx", "cy", None, "orb"),
            P("orb"),
            P("orb"),
            P("cx", "cy", "orb"),
            P("cx", "cy", None),
            P("cx", "cy", None),
            P("cx", "cy"),
            P("cx", "cy", None, None, "orb", None),
            P("cx", "cy", None, None, "orb", None),
        ),
        out_specs=P(None, "cx", "cy", None),
        check_vma=False,
    )
```

time: 72.3 us -> 58.7 us (0.81)
  the two profiles are of different devices: /device:TPU:9 before, /device:TPU:0 now
where the time goes in v3:
time: 58.7 us; the launch traced here: 58.2 us
  starting transfers between devices  19.3 us (33%)
  waiting for transfers between devices  12.1 us (21%)
  local copies, waits for them, and re-layouts  11.9 us (20%)
  Pallas kernels  11.5 us (20%)
  blocking collectives  1.83 us (3%)
  other arithmetic  0.84 us (1%)
  between operations  0.76 us (1%)
    ppermute x11, starting transfers between devices, shift(): lax.ppermute(cells, axis, [(i, (i + step) % count) for i in range(count)])  19.3 us
    ppermute x11, waiting for transfers between devices, shift(): lax.ppermute(cells, axis, [(i, (i + step) % count) for i in range(count)])  12.1 us
    pallas_call x1, Pallas kernels, per_device(): pl.pallas_call(functools.partial(own_kernel, dims), out_shape=(acc_shape,...  5.41 us
    unnamed x16, local copies, waits for them, and re-layouts  4.09 us
    squeeze x1, local copies, waits for them, and re-layouts, per_device(): high_mid = shift(coeffs[0, 1:width_y - 1], 'cx', -1)  2.61 us
    squeeze x1, local copies, waits for them, and re-layouts, per_device(): high_side = shift(after(coeffs[:, 0], high_edge), 'cy', -1)  2.28 us
    pallas_call x1, Pallas kernels, per_device(): pl.pallas_call(functools.partial(last_kernel, dims), out_shape=jax.ShapeD...  2.07 us
    pallas_call x1, Pallas kernels, per_device(): pl.pallas_call(functools.partial(side_kernel, dims), out_shape=acc_shape,...  2.02 us
  transfers between devices with their start and end apart: 11, of which 6 were waited for; matrix products, arithmetic and copies ran while one was open for 14% of the time, Pallas kernels for 16%

profile of v3, /device:TPU:0, one launch (start us, length us, event | category | flops | bytes accessed | tf_op | source)
XLA Modules:
  0.0 58.2 jit_solution(10066094883476247487)
XLA Ops:
  0.5 1.9 %slice_bitcast_fusion.4 = (bf16[2,128,512]{2,1,0:T(8,128)(2,1)}, bf16[2,128,512]{2,1,0:T(8,128)(2,1)}) fusion(bf16[4,8,128,512]{3,2,1,0:T(8,128)(2,1)} %param.9), kind=kLoop, calls=%fused_computation.6 | loop fusion | bytes 1048576 | tf_op jit(solution)/shard_map/squeeze | solution.py:228
  2.4 3.0 %collective-permute-start.2 = (bf16[2,128,512]{2,1,0:T(8,128)(2,1)}, bf16[2,128,512]{2,1,0:T(8,128)(2,1)S(1)}, u32[]{:S(2)}, u32[]{:S(2)}) collective-permute-start(bf16[2,128,512]{2,1,0:T(8,128)(2,1)} %get-tuple-element.18), channel_id=1, source_target_pairs={{0,8},{8,16},{16,24},{24,0},{1,9},{9,17},{17,25},{25,1},{2,10},{10... | collective-permute-start | bytes 786440 | tf_op jit(solution)/shard_map/ppermute | solution.py:20
  5.4 2.1 %collective-permute-start.4 = (bf16[2,128,512]{2,1,0:T(8,128)(2,1)}, bf16[2,128,512]{2,1,0:T(8,128)(2,1)}, u32[]{:S(2)}, u32[]{:S(2)}) collective-permute-start(bf16[2,128,512]{2,1,0:T(8,128)(2,1)} %get-tuple-element.17), channel_id=1, source_target_pairs={{0,24},{8,0},{16,8},{24,16},{1,25},{9,1},{17,9},{25,17},{2,26},{10... | collective-permute-start | bytes 786440 | tf_op jit(solution)/shard_map/ppermute | solution.py:20
  7.5 2.6 %slice_bitcast_fusion = (bf16[6,128,512]{2,1,0:T(8,128)(2,1)}, bf16[6,128,512]{2,1,0:T(8,128)(2,1)}) fusion(bf16[4,8,128,512]{3,2,1,0:T(8,128)(2,1)} %param.9), kind=kLoop, calls=%fused_computation | loop fusion | bytes 3145728 | tf_op jit(solution)/shard_map/squeeze | solution.py:232
  10.9 2.3 %slice_bitcast_fusion.2 = (bf16[4,128,512]{2,1,0:T(8,128)(2,1)}, bf16[4,128,512]{2,1,0:T(8,128)(2,1)}) fusion(bf16[4,8,128,512]{3,2,1,0:T(8,128)(2,1)} %param.9), kind=kLoop, calls=%fused_computation.2 | loop fusion | bytes 2097152 | tf_op jit(solution)/shard_map/squeeze | solution.py:231
  13.2 1.6 %collective-permute-done.2.rest_2_ = bf16[2,128,512]{2,1,0:T(8,128)(2,1)S(1)} collective-permute-done((bf16[2,128,512]{2,1,0:T(8,128)(2,1)}, bf16[2,128,512]{2,1,0:T(8,128)(2,1)S(1)}, u32[]{:S(2)}, u32[]{:S(2)}) %collective-permute-start.2) | collective-permute-done | bytes 262176 | tf_op jit(solution)/shard_map/ppermute | solution.py:20
  14.8 1.7 %collective-permute-start.3 = (bf16[4,128,512]{2,1,0:T(8,128)(2,1)}, bf16[4,128,512]{2,1,0:T(8,128)(2,1)}, u32[]{:S(2)}, u32[]{:S(2)}) collective-permute-start(bf16[4,128,512]{2,1,0:T(8,128)(2,1)} %get-tuple-element.13), channel_id=1, source_target_pairs={{0,2},{2,4},{4,6},{6,0},{1,3},{3,5},{5,7},{7,1},{8,10},{10,12},{12... | collective-permute-start | bytes 1572872 | tf_op jit(solution)/shard_map/ppermute | solution.py:20
  16.6 2.0 %shard_map.91.table = s32[584]{0:T(1024)S(1)} custom-call(s32[64]{0:T(128)S(1)} %bitcast.49, s32[64]{0:T(128)S(1)} %bitcast.50, s32[2]{0:T(128)S(1)} %pad_add_fusion.1.meta), custom_call_target="tpu_custom_call" | custom-call | tf_op jit(solution)/shard_map/pallas_call | solution.py:259
  18.6 1.8 %all_gather.3 = s32[2,32,64]{2,1,0:T(8,128)S(1)} all-gather(s32[1,32,64]{2,1,0:T(8,128)S(1)} %bitcast.51), channel_id=1, replica_groups=mesh['cx'=4,'cy'=4,'orb'=2] {'orb'}, dimensions={0}, use_global_device_ids=true | all-gather | bytes 24576 | tf_op jit(solution)/shard_map/all_gather | solution.py:238
  20.5 7.4 %collective-permute-start.7 = (bf16[6,128,512]{2,1,0:T(8,128)(2,1)}, bf16[6,128,512]{2,1,0:T(8,128)(2,1)S(1)}, u32[]{:S(2)}, u32[]{:S(2)}) collective-permute-start(bf16[6,128,512]{2,1,0:T(8,128)(2,1)} %get-tuple-element.15), channel_id=1, source_target_pairs={{0,24},{8,0},{16,8},{24,16},{1,25},{9,1},{17,9},{25,17},{2,26},{10... | collective-permute-start | bytes 2359304 | tf_op jit(solution)/shard_map/ppermute | solution.py:20
  27.9 0.9 %collective-permute-done.3.rest_0_ = bf16[4,128,512]{2,1,0:T(8,128)(2,1)} collective-permute-done((bf16[4,128,512]{2,1,0:T(8,128)(2,1)}, bf16[4,128,512]{2,1,0:T(8,128)(2,1)}, u32[]{:S(2)}, u32[]{:S(2)}) %collective-permute-start.3) | collective-permute-done | bytes 524320 | tf_op jit(solution)/shard_map/ppermute | solution.py:20
  28.8 1.3 %collective-permute-start.5 = (bf16[4,128,512]{2,1,0:T(8,128)(2,1)}, bf16[4,128,512]{2,1,0:T(8,128)(2,1)S(1)}, u32[]{:S(2)}, u32[]{:S(2)}) collective-permute-start(bf16[4,128,512]{2,1,0:T(8,128)(2,1)} %get-tuple-element.14), channel_id=1, source_target_pairs={{0,6},{2,0},{4,2},{6,4},{1,7},{3,1},{5,3},{7,5},{8,14},{10,8},{12,... | collective-permute-start | bytes 1572872 | tf_op jit(solution)/shard_map/ppermute | solution.py:20
  30.1 1.0 %fusion.2 = (bf16[1,128,512]{2,1,0:T(8,128)(2,1)S(1)}, bf16[1,128,512]{2,1,0:T(8,128)(2,1)S(1)}) fusion(bf16[2,128,512]{2,1,0:T(8,128)(2,1)} %collective-permute-done.4.rest_3_), kind=kLoop, calls=%fused_computation.14 | loop fusion | bytes 524288 | tf_op jit(solution)/shard_map/slice | solution.py:234
  31.2 0.8 %collective-permute-start.8 = (bf16[2,128,512]{2,1,0:T(8,128)(2,1)S(1)}, bf16[2,128,512]{2,1,0:T(8,128)(2,1)S(1)}, u32[]{:S(2)}, u32[]{:S(2)}) collective-permute-start(bf16[2,128,512]{2,1,0:T(8,128)(2,1)S(1)} %pad_maximum_fusion), channel_id=1, source_target_pairs={{0,2},{2,4},{4,6},{6,0},{1,3},{3,5},{5,7},{7,1},{8,10},{10,12},{12... | collective-permute-start | bytes 786440 | tf_op jit(solution)/shard_map/ppermute | solution.py:20
  32.0 2.2 %collective-permute-start.9 = (bf16[2,128,512]{2,1,0:T(8,128)(2,1)S(1)}, bf16[2,128,512]{2,1,0:T(8,128)(2,1)S(1)}, u32[]{:S(2)}, u32[]{:S(2)}) collective-permute-start(bf16[2,128,512]{2,1,0:T(8,128)(2,1)S(1)} %pad_maximum_fusion.1), channel_id=1, source_target_pairs={{0,6},{2,0},{4,2},{6,4},{1,7},{3,1},{5,3},{7,5},{8,14},{10,8},{12,... | collective-permute-start | bytes 786440 | tf_op jit(solution)/shard_map/ppermute | solution.py:20
  34.3 2.2 %copy-done = bf16[4,8,128,512]{3,2,1,0:T(8,128)(2,1)S(1)} copy-done((bf16[4,8,128,512]{3,2,1,0:T(8,128)(2,1)S(1)}, bf16[4,8,128,512]{3,2,1,0:T(8,128)(2,1)}, u32[]{:S(2)}) %copy-start) | copy-done | bytes 4194328
  36.5 1.9 %copy-done.2 = bf16[1,1,64,3,64,128]{5,4,3,2,1,0:T(8,128)(2,1)S(1)} copy-done((bf16[1,1,64,3,64,128]{5,4,3,2,1,0:T(8,128)(2,1)S(1)}, bf16[1,1,64,3,64,128]{5,4,3,2,1,0:T(8,128)(2,1)}, u32[]{:S(2)}) %copy-start.2) | copy-done | bytes 3145752
  38.4 5.4 %shard_map.92 = (f32[32,8,384]{2,1,0:T(8,128)S(1)}, bf16[64,3,64,128]{3,2,1,0:T(8,128)(2,1)S(1)}, bf16[64,3,64,128]{3,2,1,0:T(8,128)(2,1)S(1)}) custom-call(s32[584]{0:T(1024)S(1)} %shard_map.91.table, bf16[32,128,512]{2,1,0:T(8,128)(2,1)S(1)} %bitcast.32, bf16[64,3,64,128]{3,2,1,0:T(8,128)(2,1)S(1)} %bitcast.36, bf16[64,3,64,128]{3,2,1,0:T(8,128)(2,1)S(1)} %bitcast.40, ...), custom_call_target="tpu_custom_call" | custom-call | flops 1610612736 | bytes 22020096 | tf_op jit(solution)/shard_map/pallas_call | solution.py:266
  43.8 2.0 %shard_map.93.before = f32[32,8,384]{2,1,0:T(8,128)S(1)} custom-call(s32[584]{0:T(1024)S(1)} %shard_map.91.table, bf16[32,128,512]{2,1,0:T(8,128)(2,1)S(1)} %bitcast.33, bf16[64,3,64,128]{3,2,1,0:T(8,128)(2,1)S(1)} %bitcast.37, bf16[64,3,64,128]{3,2,1,0:T(8,128)(2,1)S(1)} %get-tuple-element.10.gh2, bf16[64,3,64,128]{3,2,1,0:T(8,128)(2,1)S(1)} %bitcast.41, ...), custom_call_target="tpu_custom_call" | custom-call | flops 301989888 | bytes 4128768 | tf_op jit(solution)/shard_map/pallas_call | solution.py:282
  45.9 4.4 %collective-permute-done.8.rest_2_ = bf16[2,128,512]{2,1,0:T(8,128)(2,1)S(1)} collective-permute-done((bf16[2,128,512]{2,1,0:T(8,128)(2,1)S(1)}, bf16[2,128,512]{2,1,0:T(8,128)(2,1)S(1)}, u32[]{:S(2)}, u32[]{:S(2)}) %collective-permute-start.8) | collective-permute-done | bytes 262176 | tf_op jit(solution)/shard_map/ppermute | solution.py:20
  50.2 3.9 %collective-permute-done.9.rest_3_ = bf16[2,128,512]{2,1,0:T(8,128)(2,1)S(1)} collective-permute-done((bf16[2,128,512]{2,1,0:T(8,128)(2,1)S(1)}, bf16[2,128,512]{2,1,0:T(8,128)(2,1)S(1)}, u32[]{:S(2)}, u32[]{:S(2)}) %collective-permute-start.9) | collective-permute-done | bytes 262176 | tf_op jit(solution)/shard_map/ppermute | solution.py:20
  54.2 2.1 %shard_map.94 = f32[3,32,8]{2,1,0:T(8,128)S(1)} custom-call(s32[584]{0:T(1024)S(1)} %shard_map.91.table, bf16[32,128,512]{2,1,0:T(8,128)(2,1)S(1)} %bitcast.34, bf16[64,3,64,128]{3,2,1,0:T(8,128)(2,1)S(1)} %bitcast.38, bf16[64,3,64,128]{3,2,1,0:T(8,128)(2,1)S(1)} %get-tuple-element.10.gh2, bf16[64,3,64,128]{3,2,1,0:T(8,128)(2,1)S(1)} %bitcast.42, ...), custom_call_target="tpu_custom_call" | custom-call | flops 201326592 | bytes 2752512 | tf_op jit(solution)/shard_map/pallas_call | solution.py:294
  56.3 1.2 %collective-permute-done.10 = f32[3,32,8]{2,1,0:T(8,128)S(1)} collective-permute-done((f32[3,32,8]{2,1,0:T(8,128)S(1)}, f32[3,32,8]{2,1,0:T(8,128)S(1)}, u32[]{:S(2)}, u32[]{:S(2)}) %collective-permute-start.10) | collective-permute-done | bytes 3104 | tf_op jit(solution)/shard_map/ppermute | solution.py:20
  57.6 0.6 %add_bitcast_fusion = f32[3,4,8,8]{3,2,1,0:T(8,128)} fusion(f32[3,32,8]{2,1,0:T(8,128)S(1)} %shard_map.94, f32[3,32,8]{2,1,0:T(8,128)S(1)} %collective-permute-done.10), kind=kLoop, calls=%fused_computation.8 | loop fusion | flops 768 | bytes 9216 | tf_op jit(solution)/shard_map/reshape | solution.py:304
  (30 shorter events, 1.1 us)
Async XLA Ops:
  0.0 31.2 %collective-permute-start = (bf16[64,3,64,128]{3,2,1,0:T(8,128)(2,1)}, bf16[64,3,64,128]{3,2,1,0:T(8,128)(2,1)}, u32[]{:S(2)}, u32[]{:S(2)}) collective-permute-start(bf16[64,3,64,128]{3,2,1,0:T(8,128)(2,1)} %bitcast.35), channel_id=1, source_target_pairs={{0,1},{1,0},{2,3},{3,2},{4,5},{5,4},{6,7},{7,6},{8,9},{9,8},{10,11... | collective-permute-start | bytes 9437192 | tf_op jit(solution)/shard_map/ppermute | solution.py:20
  0.5 16.2 %copy-start.5 = (s32[1,1,64]{2,1,0:T(1,128)S(1)}, s32[1,1,64]{2,1,0:T(1,128)}, u32[]{:S(2)}) copy-start(s32[1,1,64]{2,1,0:T(1,128)} %param.13) | copy-start | bytes 772
  0.5 16.2 %copy-start.6 = (s32[1,1,64]{2,1,0:T(1,128)S(1)}, s32[1,1,64]{2,1,0:T(1,128)}, u32[]{:S(2)}) copy-start(s32[1,1,64]{2,1,0:T(1,128)} %param.14) | copy-start | bytes 772
  0.5 18.2 %copy-start.7 = (s32[4,8,64]{2,1,0:T(8,128)S(1)}, s32[4,8,64]{2,1,0:T(8,128)}, u32[]{:S(2)}) copy-start(s32[4,8,64]{2,1,0:T(8,128)} %param.12) | copy-start | bytes 24580
  0.5 31.5 %collective-permute-start.1 = (bf16[64,3,64,128]{3,2,1,0:T(8,128)(2,1)}, bf16[64,3,64,128]{3,2,1,0:T(8,128)(2,1)}, u32[]{:S(2)}, u32[]{:S(2)}) collective-permute-start(bf16[64,3,64,128]{3,2,1,0:T(8,128)(2,1)} %bitcast.39), channel_id=1, source_target_pairs={{0,1},{1,0},{2,3},{3,2},{4,5},{5,4},{6,7},{7,6},{8,9},{9,8},{10,11... | collective-permute-start | bytes 9437192 | tf_op jit(solution)/shard_map/ppermute | solution.py:20
  2.4 12.4 %collective-permute-start.2 = (bf16[2,128,512]{2,1,0:T(8,128)(2,1)}, bf16[2,128,512]{2,1,0:T(8,128)(2,1)S(1)}, u32[]{:S(2)}, u32[]{:S(2)}) collective-permute-start(bf16[2,128,512]{2,1,0:T(8,128)(2,1)} %get-tuple-element.18), channel_id=1, source_target_pairs={{0,8},{8,16},{16,24},{24,0},{1,9},{9,17},{17,25},{25,1},{2,10},{10... | collective-permute-start | bytes 786440 | tf_op jit(solution)/shard_map/ppermute | solution.py:20
  5.4 28.9 %copy-start.1 = (bf16[1,1,64,3,64,128]{5,4,3,2,1,0:T(8,128)(2,1)S(1)}, bf16[1,1,64,3,64,128]{5,4,3,2,1,0:T(8,128)(2,1)}, u32[]{:S(2)}) copy-start(bf16[1,1,64,3,64,128]{5,4,3,2,1,0:T(8,128)(2,1)} %param.16) | copy-start | bytes 9437188
  5.4 28.9 %copy-start.3 = (f32[512]{0:T(512)S(1)}, f32[512]{0:T(512)}, u32[]{:S(2)}) copy-start(f32[512]{0:T(512)} %param.10) | copy-start | bytes 6148
  5.4 28.9 %copy-start.4 = (f32[512]{0:T(512)S(1)}, f32[512]{0:T(512)}, u32[]{:S(2)}) copy-start(f32[512]{0:T(512)} %param.11) | copy-start | bytes 6148
  5.4 15.1 %collective-permute-start.4 = (bf16[2,128,512]{2,1,0:T(8,128)(2,1)}, bf16[2,128,512]{2,1,0:T(8,128)(2,1)}, u32[]{:S(2)}, u32[]{:S(2)}) collective-permute-start(bf16[2,128,512]{2,1,0:T(8,128)(2,1)} %get-tuple-element.17), channel_id=1, source_target_pairs={{0,24},{8,0},{16,8},{24,16},{1,25},{9,1},{17,9},{25,17},{2,26},{10... | collective-permute-start | bytes 786440 | tf_op jit(solution)/shard_map/ppermute | solution.py:20
  10.1 44.1 %collective-permute-start.6 = (bf16[6,128,512]{2,1,0:T(8,128)(2,1)}, bf16[6,128,512]{2,1,0:T(8,128)(2,1)}, u32[]{:S(2)}, u32[]{:S(2)}) collective-permute-start(bf16[6,128,512]{2,1,0:T(8,128)(2,1)} %get-tuple-element.16), channel_id=1, source_target_pairs={{0,8},{8,16},{16,24},{24,0},{1,9},{9,17},{17,25},{25,1},{2,10},{10... | collective-permute-start | bytes 2359304 | tf_op jit(solution)/shard_map/ppermute | solution.py:20
  14.8 14.0 %collective-permute-start.3 = (bf16[4,128,512]{2,1,0:T(8,128)(2,1)}, bf16[4,128,512]{2,1,0:T(8,128)(2,1)}, u32[]{:S(2)}, u32[]{:S(2)}) collective-permute-start(bf16[4,128,512]{2,1,0:T(8,128)(2,1)} %get-tuple-element.13), channel_id=1, source_target_pairs={{0,2},{2,4},{4,6},{6,0},{1,3},{3,5},{5,7},{7,1},{8,10},{10,12},{12... | collective-permute-start | bytes 1572872 | tf_op jit(solution)/shard_map/ppermute | solution.py:20
  20.5 33.7 %collective-permute-start.7 = (bf16[6,128,512]{2,1,0:T(8,128)(2,1)}, bf16[6,128,512]{2,1,0:T(8,128)(2,1)S(1)}, u32[]{:S(2)}, u32[]{:S(2)}) collective-permute-start(bf16[6,128,512]{2,1,0:T(8,128)(2,1)} %get-tuple-element.15), channel_id=1, source_target_pairs={{0,24},{8,0},{16,8},{24,16},{1,25},{9,1},{17,9},{25,17},{2,26},{10... | collective-permute-start | bytes 2359304 | tf_op jit(solution)/shard_map/ppermute | solution.py:20
  28.8 15.0 %collective-permute-start.5 = (bf16[4,128,512]{2,1,0:T(8,128)(2,1)}, bf16[4,128,512]{2,1,0:T(8,128)(2,1)S(1)}, u32[]{:S(2)}, u32[]{:S(2)}) collective-permute-start(bf16[4,128,512]{2,1,0:T(8,128)(2,1)} %get-tuple-element.14), channel_id=1, source_target_pairs={{0,6},{2,0},{4,2},{6,4},{1,7},{3,1},{5,3},{7,5},{8,14},{10,8},{12,... | collective-permute-start | bytes 1572872 | tf_op jit(solution)/shard_map/ppermute | solution.py:20
  31.2 19.0 %collective-permute-start.8 = (bf16[2,128,512]{2,1,0:T(8,128)(2,1)S(1)}, bf16[2,128,512]{2,1,0:T(8,128)(2,1)S(1)}, u32[]{:S(2)}, u32[]{:S(2)}) collective-permute-start(bf16[2,128,512]{2,1,0:T(8,128)(2,1)S(1)} %pad_maximum_fusion), channel_id=1, source_target_pairs={{0,2},{2,4},{4,6},{6,0},{1,3},{3,5},{5,7},{7,1},{8,10},{10,12},{12... | collective-permute-start | bytes 786440 | tf_op jit(solution)/shard_map/ppermute | solution.py:20
  32.0 22.2 %collective-permute-start.9 = (bf16[2,128,512]{2,1,0:T(8,128)(2,1)S(1)}, bf16[2,128,512]{2,1,0:T(8,128)(2,1)S(1)}, u32[]{:S(2)}, u32[]{:S(2)}) collective-permute-start(bf16[2,128,512]{2,1,0:T(8,128)(2,1)S(1)} %pad_maximum_fusion.1), channel_id=1, source_target_pairs={{0,6},{2,0},{4,2},{6,4},{1,7},{3,1},{5,3},{7,5},{8,14},{10,8},{12,... | collective-permute-start | bytes 786440 | tf_op jit(solution)/shard_map/ppermute | solution.py:20
  34.3 2.2 %copy-start = (bf16[4,8,128,512]{3,2,1,0:T(8,128)(2,1)S(1)}, bf16[4,8,128,512]{3,2,1,0:T(8,128)(2,1)}, u32[]{:S(2)}) copy-start(bf16[4,8,128,512]{3,2,1,0:T(8,128)(2,1)} %param.9) | copy-start | bytes 12582916
  36.5 1.9 %copy-start.2 = (bf16[1,1,64,3,64,128]{5,4,3,2,1,0:T(8,128)(2,1)S(1)}, bf16[1,1,64,3,64,128]{5,4,3,2,1,0:T(8,128)(2,1)}, u32[]{:S(2)}) copy-start(bf16[1,1,64,3,64,128]{5,4,3,2,1,0:T(8,128)(2,1)} %param.17) | copy-start | bytes 9437188
  56.3 1.3 %collective-permute-start.10 = (f32[3,32,8]{2,1,0:T(8,128)S(1)}, f32[3,32,8]{2,1,0:T(8,128)S(1)}, u32[]{:S(2)}, u32[]{:S(2)}) collective-permute-start(f32[3,32,8]{2,1,0:T(8,128)S(1)} %shard_map.94), channel_id=1, source_target_pairs={{0,1},{1,0},{2,3},{3,2},{4,5},{5,4},{6,7},{7,6},{8,9},{9,8},{10,11... | collective-permute-start | bytes 9224 | tf_op jit(solution)/shard_map/ppermute | solution.py:20

commit v4 on v3

--- a/solution.py
+++ b/solution.py
@@ -64,11 +64,11 @@
 
 def sort_kernel(dims, first, second, meta, table):
     width_x, width_y, slots = dims
-    tail = 9 * slots
-    for k in range(3):
+    tail = 12 * slots
+    for k in range(4):
         table[tail + k] = 0
-    table[tail + 3] = meta[1]
-    table[tail + 4] = meta[0]
+    table[tail + 4] = meta[1]
+    table[tail + 5] = meta[0]
 
     def place(s, carry):
         g = second[s]
@@ -78,14 +78,17 @@
         at_end = jnp.logical_or(gy == 0, gy == width_y - 1)
         row = (gx > 0).astype(jnp.int32)
         column = (gy > 0).astype(jnp.int32)
-        stage = jnp.where(inside_x, jnp.where(inside_y, 0, 1), jnp.where(at_end, 1, 2))
+        rest = jnp.where(inside_y, 2 + row, 3)
+        stage = jnp.where(
+            inside_x, jnp.where(inside_y, 0, 1), jnp.where(at_end, 1, rest)
+        )
         spot = jnp.where(
             inside_x,
             jnp.where(inside_y, gx * width_y + gy, column * width_x + gx),
             jnp.where(
                 inside_y,
-                jnp.where(at_end, 2 * width_x + 2 * row + column, row * (width_y - 2) + gy - 1),
-                2 * (width_y - 2) + 2 * column + row,
+                jnp.where(at_end, 2 * width_x + 2 * row + column, gy - 1),
+                width_y - 2 + 2 * column + row,
             ),
         )
         used = table[tail + stage]
@@ -104,7 +107,7 @@
 ):
     slots = dims[2]
     half_rows = grads[0].shape[2]
-    number, half = table[9 * slots + stage], table[9 * slots + 3]
+    number, half = table[12 * slots + stage], table[12 * slots + 4]
     offsets = [pl.multiple_of(part * half_rows, half_rows) for part in (half, 1 - half)]
 
     def visit(i, done):
@@ -137,7 +140,7 @@
     dims, table, coeffs, gh, gs, gh_far, gs_far, occ, energy, atoms, acc, gh2, gs2, sems
 ):
     slots = dims[2]
-    chunks = (table[9 * slots + 4] + CHUNK - 1) // CHUNK
+    chunks = (table[12 * slots + 5] + CHUNK - 1) // CHUNK
 
     def copies(k):
         part = pl.ds(pl.multiple_of(k * CHUNK, CHUNK), CHUNK)
@@ -189,6 +192,15 @@
     )
 
 
+def low_kernel(
+    dims, table, coeffs, gh, gh2, gs, gs2, occ, energy, atoms, before, rim, acc
+):
+    acc[...] = before[...]
+    stage_body(
+        dims, 2, lambda spot: rim[spot], table, coeffs, (gh, gh2, gs, gs2), occ, energy, atoms, acc
+    )
+
+
 def last_kernel(
     dims, table, coeffs, gh, gh2, gs, gs2, occ, energy, atoms, before, *rest
 ):
@@ -205,7 +217,7 @@
         return cell
 
     stage_body(
-        dims, 2, right, table, coeffs, (gh, gh2, gs, gs2), occ, energy, atoms, acc
+        dims, 3, right, table, coeffs, (gh, gh2, gs, gs2), occ, energy, atoms, acc
     )
     basis = atoms.shape[1]
     for c in range(3):
@@ -258,7 +270,7 @@
 
     table = pl.pallas_call(
         functools.partial(sort_kernel, dims),
-        out_shape=jax.ShapeDtypeStruct((9 * slots + 8,), jnp.int32),
+        out_shape=jax.ShapeDtypeStruct((12 * slots + 8,), jnp.int32),
         in_specs=[SMEM] * 3,
         out_specs=SMEM,
         compiler_params=pltpu.CompilerParams(vmem_limit_bytes=1024 * 1024),
@@ -291,15 +303,23 @@
         compiler_params=params,
         cost_estimate=cost(0.15),
     )(*common, acc, *rims)
+    acc = pl.pallas_call(
+        functools.partial(low_kernel, dims),
+        out_shape=acc_shape,
+        in_specs=common_specs + [VMEM] * 2,
+        out_specs=VMEM,
+        compiler_params=params,
+        cost_estimate=cost(0.1),
+    )(*common, acc, low_mid)
     out = pl.pallas_call(
         functools.partial(last_kernel, dims),
         out_shape=jax.ShapeDtypeStruct((3, local, ATOMS), jnp.float32),
-        in_specs=common_specs + [VMEM] * 5,
+        in_specs=common_specs + [VMEM] * 4,
         out_specs=VMEM,
         scratch_shapes=[pltpu.VMEM(acc_shape.shape, jnp.float32)],
         compiler_params=params,
         cost_estimate=cost(0.1),
-    )(*common, acc, low_mid, high_mid, low_corner, high_corner)
+    )(*common, acc, high_mid, low_corner, high_corner)
     total = out + shift(out, "orb", 1)
     return total.reshape(3, width_x, width_y, ATOMS)
 

time: 58.7 us -> 58.6 us (level)
  the two profiles are of different devices: /device:TPU:0 before, /device:TPU:23 now
where the time goes in v4:
time: 58.6 us; the launch traced here: 57.9 us
  Pallas kernels  21.3 us (36%)
  local copies, waits for them, and re-layouts  12 us (20%)
  starting transfers between devices  11.2 us (19%)
  blocking collectives  8.88 us (15%)
  waiting for transfers between devices  2.83 us (5%)
  other arithmetic  0.84 us (1%)
  between operations  0.81 us (1%)
    ppermute x11, starting transfers between devices, shift(): lax.ppermute(cells, axis, [(i, (i + step) % count) for i in range(count)])  11.2 us
    pallas_call x1, Pallas kernels, per_device(): pl.pallas_call(functools.partial(own_kernel, dims), out_shape=(acc_shape,...  10.4 us
    all_gather x1, blocking collectives, per_device(): atoms_all = lax.all_gather(atoms_own, 'orb', axis=0)  8.88 us
    unnamed x16, local copies, waits for them, and re-layouts  4.09 us
    pallas_call x1, Pallas kernels, per_device(): pl.pallas_call(functools.partial(side_kernel, dims), out_shape=acc_shape,...  3.45 us
    pallas_call x1, Pallas kernels, per_device(): pl.pallas_call(functools.partial(sort_kernel, dims), out_shape=jax.ShapeD...  3.29 us
    ppermute x11, waiting for transfers between devices, shift(): lax.ppermute(cells, axis, [(i, (i + step) % count) for i in range(count)])  2.83 us
    squeeze x1, local copies, waits for them, and re-layouts, per_device(): high_mid = shift(coeffs[0, 1:width_y - 1], 'cx', -1)  2.76 us
  transfers between devices with their start and end apart: 11, of which 2 were waited for; matrix products, arithmetic and copies ran while one was open for 14% of the time, Pallas kernels for 34%

profile of v4, /device:TPU:23, one launch (start us, length us, event | category | flops | bytes accessed | tf_op | source)
XLA Modules:
  0.0 57.9 jit_solution(543857401858228556)
XLA Ops:
  0.0 0.7 %collective-permute-start = (bf16[64,3,64,128]{3,2,1,0:T(8,128)(2,1)}, bf16[64,3,64,128]{3,2,1,0:T(8,128)(2,1)}, u32[]{:S(2)}, u32[]{:S(2)}) collective-permute-start(bf16[64,3,64,128]{3,2,1,0:T(8,128)(2,1)} %bitcast.36), channel_id=1, source_target_pairs={{0,1},{1,0},{2,3},{3,2},{4,5},{5,4},{6,7},{7,6},{8,9},{9,8},{10,11... | collective-permute-start | bytes 9437192 | tf_op jit(solution)/shard_map/ppermute | solution.py:20
  0.7 0.1 collective-permute-start.1
  0.8 1.9 %slice_bitcast_fusion.4 = (bf16[2,128,512]{2,1,0:T(8,128)(2,1)}, bf16[2,128,512]{2,1,0:T(8,128)(2,1)}) fusion(bf16[4,8,128,512]{3,2,1,0:T(8,128)(2,1)} %param.9), kind=kLoop, calls=%fused_computation.6 | loop fusion | bytes 1048576 | tf_op jit(solution)/shard_map/squeeze | solution.py:240
  2.6 1.3 %collective-permute-start.2 = (bf16[2,128,512]{2,1,0:T(8,128)(2,1)}, bf16[2,128,512]{2,1,0:T(8,128)(2,1)S(1)}, u32[]{:S(2)}, u32[]{:S(2)}) collective-permute-start(bf16[2,128,512]{2,1,0:T(8,128)(2,1)} %get-tuple-element.18), channel_id=1, source_target_pairs={{0,8},{8,16},{16,24},{24,0},{1,9},{9,17},{17,25},{25,1},{2,10},{10... | collective-permute-start | bytes 786440 | tf_op jit(solution)/shard_map/ppermute | solution.py:20
  3.9 0.2 collective-permute-start.4
  4.1 2.8 %slice_bitcast_fusion = (bf16[6,128,512]{2,1,0:T(8,128)(2,1)}, bf16[6,128,512]{2,1,0:T(8,128)(2,1)}) fusion(bf16[4,8,128,512]{3,2,1,0:T(8,128)(2,1)} %param.9), kind=kLoop, calls=%fused_computation | loop fusion | bytes 3145728 | tf_op jit(solution)/shard_map/squeeze | solution.py:244
  6.9 1.1 %collective-permute-start.6 = (bf16[6,128,512]{2,1,0:T(8,128)(2,1)}, bf16[6,128,512]{2,1,0:T(8,128)(2,1)}, u32[]{:S(2)}, u32[]{:S(2)}) collective-permute-start(bf16[6,128,512]{2,1,0:T(8,128)(2,1)} %get-tuple-element.16), channel_id=1, source_target_pairs={{0,8},{8,16},{16,24},{24,0},{1,9},{9,17},{17,25},{25,1},{2,10},{10... | collective-permute-start | bytes 2359304 | tf_op jit(solution)/shard_map/ppermute | solution.py:20
  8.7 2.3 %slice_bitcast_fusion.2 = (bf16[4,128,512]{2,1,0:T(8,128)(2,1)}, bf16[4,128,512]{2,1,0:T(8,128)(2,1)}) fusion(bf16[4,8,128,512]{3,2,1,0:T(8,128)(2,1)} %param.9), kind=kLoop, calls=%fused_computation.2 | loop fusion | bytes 2097152 | tf_op jit(solution)/shard_map/squeeze | solution.py:243
  10.9 0.2 collective-permute-start.3
  11.2 3.3 %shard_map.91.table = s32[776]{0:T(1024)S(1)} custom-call(s32[64]{0:T(128)S(1)} %bitcast.54, s32[64]{0:T(128)S(1)} %bitcast.55, s32[2]{0:T(128)S(1)} %pad_add_fusion.1.meta), custom_call_target="tpu_custom_call" | custom-call | tf_op jit(solution)/shard_map/pallas_call | solution.py:271
  14.5 8.9 %all_gather.3 = s32[2,32,64]{2,1,0:T(8,128)S(1)} all-gather(s32[1,32,64]{2,1,0:T(8,128)S(1)} %bitcast.56), channel_id=1, replica_groups=mesh['cx'=4,'cy'=4,'orb'=2] {'orb'}, dimensions={0}, use_global_device_ids=true | all-gather | bytes 24576 | tf_op jit(solution)/shard_map/all_gather | solution.py:250
  23.5 0.3 collective-permute-start.5
  23.8 1.0 %fusion.2 = (bf16[1,128,512]{2,1,0:T(8,128)(2,1)S(1)}, bf16[1,128,512]{2,1,0:T(8,128)(2,1)S(1)}) fusion(bf16[2,128,512]{2,1,0:T(8,128)(2,1)} %collective-permute-done.4.rest_3_), kind=kLoop, calls=%fused_computation.14 | loop fusion | bytes 524288 | tf_op jit(solution)/shard_map/slice | solution.py:246
  24.8 2.2 %collective-permute-start.8 = (bf16[2,128,512]{2,1,0:T(8,128)(2,1)S(1)}, bf16[2,128,512]{2,1,0:T(8,128)(2,1)S(1)}, u32[]{:S(2)}, u32[]{:S(2)}) collective-permute-start(bf16[2,128,512]{2,1,0:T(8,128)(2,1)S(1)} %pad_maximum_fusion), channel_id=1, source_target_pairs={{0,2},{2,4},{4,6},{6,0},{1,3},{3,5},{5,7},{7,1},{8,10},{10,12},{12... | collective-permute-start | bytes 786440 | tf_op jit(solution)/shard_map/ppermute | solution.py:20
  27.1 2.2 %copy-done = bf16[4,8,128,512]{3,2,1,0:T(8,128)(2,1)S(1)} copy-done((bf16[4,8,128,512]{3,2,1,0:T(8,128)(2,1)S(1)}, bf16[4,8,128,512]{3,2,1,0:T(8,128)(2,1)}, u32[]{:S(2)}) %copy-start) | copy-done | bytes 4194328
  29.3 1.9 %copy-done.2 = bf16[1,1,64,3,64,128]{5,4,3,2,1,0:T(8,128)(2,1)S(1)} copy-done((bf16[1,1,64,3,64,128]{5,4,3,2,1,0:T(8,128)(2,1)S(1)}, bf16[1,1,64,3,64,128]{5,4,3,2,1,0:T(8,128)(2,1)}, u32[]{:S(2)}) %copy-start.2) | copy-done | bytes 3145752
  31.2 10.4 %shard_map.92 = (f32[32,8,384]{2,1,0:T(8,128)S(1)}, bf16[64,3,64,128]{3,2,1,0:T(8,128)(2,1)S(1)}, bf16[64,3,64,128]{3,2,1,0:T(8,128)(2,1)S(1)}) custom-call(s32[776]{0:T(1024)S(1)} %shard_map.91.table, bf16[32,128,512]{2,1,0:T(8,128)(2,1)S(1)} %bitcast.32, bf16[64,3,64,128]{3,2,1,0:T(8,128)(2,1)S(1)} %bitcast.37, bf16[64,3,64,128]{3,2,1,0:T(8,128)(2,1)S(1)} %bitcast.42, ...), custom_call_target="tpu_custom_call" | custom-call | flops 1610612736 | bytes 22020096 | tf_op jit(solution)/shard_map/pallas_call | solution.py:278
  41.7 3.4 %shard_map.93.before = f32[32,8,384]{2,1,0:T(8,128)S(1)} custom-call(s32[776]{0:T(1024)S(1)} %shard_map.91.table, bf16[32,128,512]{2,1,0:T(8,128)(2,1)S(1)} %bitcast.33, bf16[64,3,64,128]{3,2,1,0:T(8,128)(2,1)S(1)} %bitcast.38, bf16[64,3,64,128]{3,2,1,0:T(8,128)(2,1)S(1)} %get-tuple-element.10.gh2, bf16[64,3,64,128]{3,2,1,0:T(8,128)(2,1)S(1)} %bitcast.43, ...), custom_call_target="tpu_custom_call" | custom-call | flops 301989888 | bytes 4128768 | tf_op jit(solution)/shard_map/pallas_call | solution.py:294
  45.1 2.6 %shard_map.94.before = f32[32,8,384]{2,1,0:T(8,128)S(1)} custom-call(s32[776]{0:T(1024)S(1)} %shard_map.91.table, bf16[32,128,512]{2,1,0:T(8,128)(2,1)S(1)} %bitcast.34, bf16[64,3,64,128]{3,2,1,0:T(8,128)(2,1)S(1)} %bitcast.39, bf16[64,3,64,128]{3,2,1,0:T(8,128)(2,1)S(1)} %get-tuple-element.10.gh2, bf16[64,3,64,128]{3,2,1,0:T(8,128)(2,1)S(1)} %bitcast.44, ...), custom_call_target="tpu_custom_call" | custom-call | flops 201326592 | bytes 2752512 | tf_op jit(solution)/shard_map/pallas_call | solution.py:306
  47.7 1.9 %collective-permute-done.7.rest_0_ = bf16[6,128,512]{2,1,0:T(8,128)(2,1)S(1)} collective-permute-done((bf16[6,128,512]{2,1,0:T(8,128)(2,1)}, bf16[6,128,512]{2,1,0:T(8,128)(2,1)S(1)}, u32[]{:S(2)}, u32[]{:S(2)}) %collective-permute-start.7) | collective-permute-done | bytes 786464 | tf_op jit(solution)/shard_map/ppermute | solution.py:20
  49.6 1.5 %shard_map.95 = f32[3,32,8]{2,1,0:T(8,128)S(1)} custom-call(s32[776]{0:T(1024)S(1)} %shard_map.91.table, bf16[32,128,512]{2,1,0:T(8,128)(2,1)S(1)} %bitcast.35, bf16[64,3,64,128]{3,2,1,0:T(8,128)(2,1)S(1)} %bitcast.40, bf16[64,3,64,128]{3,2,1,0:T(8,128)(2,1)S(1)} %get-tuple-element.10.gh2, bf16[64,3,64,128]{3,2,1,0:T(8,128)(2,1)S(1)} %bitcast.45, ...), custom_call_target="tpu_custom_call" | custom-call | flops 201326592 | bytes 2752512 | tf_op jit(solution)/shard_map/pallas_call | solution.py:314
  51.2 5.2 %collective-permute-start.10 = (f32[3,32,8]{2,1,0:T(8,128)S(1)}, f32[3,32,8]{2,1,0:T(8,128)S(1)}, u32[]{:S(2)}, u32[]{:S(2)}) collective-permute-start(f32[3,32,8]{2,1,0:T(8,128)S(1)} %shard_map.95), channel_id=1, source_target_pairs={{0,1},{1,0},{2,3},{3,2},{4,5},{5,4},{6,7},{7,6},{8,9},{9,8},{10,11... | collective-permute-start | bytes 9224 | tf_op jit(solution)/shard_map/ppermute | solution.py:20
  56.4 0.9 %collective-permute-done.10 = f32[3,32,8]{2,1,0:T(8,128)S(1)} collective-permute-done((f32[3,32,8]{2,1,0:T(8,128)S(1)}, f32[3,32,8]{2,1,0:T(8,128)S(1)}, u32[]{:S(2)}, u32[]{:S(2)}) %collective-permute-start.10) | collective-permute-done | bytes 3104 | tf_op jit(solution)/shard_map/ppermute | solution.py:20
  57.2 0.6 %add_bitcast_fusion = f32[3,4,8,8]{3,2,1,0:T(8,128)} fusion(f32[3,32,8]{2,1,0:T(8,128)S(1)} %shard_map.95, f32[3,32,8]{2,1,0:T(8,128)S(1)} %collective-permute-done.10), kind=kLoop, calls=%fused_computation.8 | loop fusion | flops 768 | bytes 9216 | tf_op jit(solution)/shard_map/reshape | solution.py:324
  (31 shorter events, 0.3 us)
Async XLA Ops:
  0.0 24.8 %collective-permute-start = (bf16[64,3,64,128]{3,2,1,0:T(8,128)(2,1)}, bf16[64,3,64,128]{3,2,1,0:T(8,128)(2,1)}, u32[]{:S(2)}, u32[]{:S(2)}) collective-permute-start(bf16[64,3,64,128]{3,2,1,0:T(8,128)(2,1)} %bitcast.36), channel_id=1, source_target_pairs={{0,1},{1,0},{2,3},{3,2},{4,5},{5,4},{6,7},{7,6},{8,9},{9,8},{10,11... | collective-permute-start | bytes 9437192 | tf_op jit(solution)/shard_map/ppermute | solution.py:20
  0.7 10.6 %copy-start.5 = (s32[1,1,64]{2,1,0:T(1,128)S(1)}, s32[1,1,64]{2,1,0:T(1,128)}, u32[]{:S(2)}) copy-start(s32[1,1,64]{2,1,0:T(1,128)} %param.13) | copy-start | bytes 772
  0.7 10.6 %copy-start.6 = (s32[1,1,64]{2,1,0:T(1,128)S(1)}, s32[1,1,64]{2,1,0:T(1,128)}, u32[]{:S(2)}) copy-start(s32[1,1,64]{2,1,0:T(1,128)} %param.14) | copy-start | bytes 772
  0.7 13.8 %copy-start.7 = (s32[4,8,64]{2,1,0:T(8,128)S(1)}, s32[4,8,64]{2,1,0:T(8,128)}, u32[]{:S(2)}) copy-start(s32[4,8,64]{2,1,0:T(8,128)} %param.12) | copy-start | bytes 24580
  0.7 26.3 %collective-permute-start.1 = (bf16[64,3,64,128]{3,2,1,0:T(8,128)(2,1)}, bf16[64,3,64,128]{3,2,1,0:T(8,128)(2,1)}, u32[]{:S(2)}, u32[]{:S(2)}) collective-permute-start(bf16[64,3,64,128]{3,2,1,0:T(8,128)(2,1)} %bitcast.41), channel_id=1, source_target_pairs={{0,1},{1,0},{2,3},{3,2},{4,5},{5,4},{6,7},{7,6},{8,9},{9,8},{10,11... | collective-permute-start | bytes 9437192 | tf_op jit(solution)/shard_map/ppermute | solution.py:20
  2.6 8.3 %collective-permute-start.2 = (bf16[2,128,512]{2,1,0:T(8,128)(2,1)}, bf16[2,128,512]{2,1,0:T(8,128)(2,1)S(1)}, u32[]{:S(2)}, u32[]{:S(2)}) collective-permute-start(bf16[2,128,512]{2,1,0:T(8,128)(2,1)} %get-tuple-element.18), channel_id=1, source_target_pairs={{0,8},{8,16},{16,24},{24,0},{1,9},{9,17},{17,25},{25,1},{2,10},{10... | collective-permute-start | bytes 786440 | tf_op jit(solution)/shard_map/ppermute | solution.py:20
  3.9 23.2 %copy-start.1 = (bf16[1,1,64,3,64,128]{5,4,3,2,1,0:T(8,128)(2,1)S(1)}, bf16[1,1,64,3,64,128]{5,4,3,2,1,0:T(8,128)(2,1)}, u32[]{:S(2)}) copy-start(bf16[1,1,64,3,64,128]{5,4,3,2,1,0:T(8,128)(2,1)} %param.16) | copy-start | bytes 9437188
  3.9 23.2 %copy-start.3 = (f32[512]{0:T(512)S(1)}, f32[512]{0:T(512)}, u32[]{:S(2)}) copy-start(f32[512]{0:T(512)} %param.10) | copy-start | bytes 6148
  3.9 23.2 %copy-start.4 = (f32[512]{0:T(512)S(1)}, f32[512]{0:T(512)}, u32[]{:S(2)}) copy-start(f32[512]{0:T(512)} %param.11) | copy-start | bytes 6148
  3.9 19.5 %collective-permute-start.4 = (bf16[2,128,512]{2,1,0:T(8,128)(2,1)}, bf16[2,128,512]{2,1,0:T(8,128)(2,1)}, u32[]{:S(2)}, u32[]{:S(2)}) collective-permute-start(bf16[2,128,512]{2,1,0:T(8,128)(2,1)} %get-tuple-element.17), channel_id=1, source_target_pairs={{0,24},{8,0},{16,8},{24,16},{1,25},{9,1},{17,9},{25,17},{2,26},{10... | collective-permute-start | bytes 786440 | tf_op jit(solution)/shard_map/ppermute | solution.py:20
  6.9 38.2 %collective-permute-start.6 = (bf16[6,128,512]{2,1,0:T(8,128)(2,1)}, bf16[6,128,512]{2,1,0:T(8,128)(2,1)}, u32[]{:S(2)}, u32[]{:S(2)}) collective-permute-start(bf16[6,128,512]{2,1,0:T(8,128)(2,1)} %get-tuple-element.16), channel_id=1, source_target_pairs={{0,8},{8,16},{16,24},{24,0},{1,9},{9,17},{17,25},{25,1},{2,10},{10... | collective-permute-start | bytes 2359304 | tf_op jit(solution)/shard_map/ppermute | solution.py:20
  10.9 12.5 %collective-permute-start.3 = (bf16[4,128,512]{2,1,0:T(8,128)(2,1)}, bf16[4,128,512]{2,1,0:T(8,128)(2,1)}, u32[]{:S(2)}, u32[]{:S(2)}) collective-permute-start(bf16[4,128,512]{2,1,0:T(8,128)(2,1)} %get-tuple-element.13), channel_id=1, source_target_pairs={{0,2},{2,4},{4,6},{6,0},{1,3},{3,5},{5,7},{7,1},{8,10},{10,12},{12... | collective-permute-start | bytes 1572872 | tf_op jit(solution)/shard_map/ppermute | solution.py:20
  23.4 26.2 %collective-permute-start.7 = (bf16[6,128,512]{2,1,0:T(8,128)(2,1)}, bf16[6,128,512]{2,1,0:T(8,128)(2,1)S(1)}, u32[]{:S(2)}, u32[]{:S(2)}) collective-permute-start(bf16[6,128,512]{2,1,0:T(8,128)(2,1)} %get-tuple-element.15), channel_id=1, source_target_pairs={{0,24},{8,0},{16,8},{24,16},{1,25},{9,1},{17,9},{25,17},{2,26},{10... | collective-permute-start | bytes 2359304 | tf_op jit(solution)/shard_map/ppermute | solution.py:20
  23.5 18.2 %collective-permute-start.5 = (bf16[4,128,512]{2,1,0:T(8,128)(2,1)}, bf16[4,128,512]{2,1,0:T(8,128)(2,1)S(1)}, u32[]{:S(2)}, u32[]{:S(2)}) collective-permute-start(bf16[4,128,512]{2,1,0:T(8,128)(2,1)} %get-tuple-element.14), channel_id=1, source_target_pairs={{0,6},{2,0},{4,2},{6,4},{1,7},{3,1},{5,3},{7,5},{8,14},{10,8},{12,... | collective-permute-start | bytes 1572872 | tf_op jit(solution)/shard_map/ppermute | solution.py:20
  24.8 22.9 %collective-permute-start.8 = (bf16[2,128,512]{2,1,0:T(8,128)(2,1)S(1)}, bf16[2,128,512]{2,1,0:T(8,128)(2,1)S(1)}, u32[]{:S(2)}, u32[]{:S(2)}) collective-permute-start(bf16[2,128,512]{2,1,0:T(8,128)(2,1)S(1)} %pad_maximum_fusion), channel_id=1, source_target_pairs={{0,2},{2,4},{4,6},{6,0},{1,3},{3,5},{5,7},{7,1},{8,10},{10,12},{12... | collective-permute-start | bytes 786440 | tf_op jit(solution)/shard_map/ppermute | solution.py:20
  27.0 20.7 %collective-permute-start.9 = (bf16[2,128,512]{2,1,0:T(8,128)(2,1)S(1)}, bf16[2,128,512]{2,1,0:T(8,128)(2,1)S(1)}, u32[]{:S(2)}, u32[]{:S(2)}) collective-permute-start(bf16[2,128,512]{2,1,0:T(8,128)(2,1)S(1)} %pad_maximum_fusion.1), channel_id=1, source_target_pairs={{0,6},{2,0},{4,2},{6,4},{1,7},{3,1},{5,3},{7,5},{8,14},{10,8},{12,... | collective-permute-start | bytes 786440 | tf_op jit(solution)/shard_map/ppermute | solution.py:20
  27.1 2.2 %copy-start = (bf16[4,8,128,512]{3,2,1,0:T(8,128)(2,1)S(1)}, bf16[4,8,128,512]{3,2,1,0:T(8,128)(2,1)}, u32[]{:S(2)}) copy-start(bf16[4,8,128,512]{3,2,1,0:T(8,128)(2,1)} %param.9) | copy-start | bytes 12582916
  29.3 1.9 %copy-start.2 = (bf16[1,1,64,3,64,128]{5,4,3,2,1,0:T(8,128)(2,1)S(1)}, bf16[1,1,64,3,64,128]{5,4,3,2,1,0:T(8,128)(2,1)}, u32[]{:S(2)}) copy-start(bf16[1,1,64,3,64,128]{5,4,3,2,1,0:T(8,128)(2,1)} %param.17) | copy-start | bytes 9437188
  51.2 6.1 %collective-permute-start.10 = (f32[3,32,8]{2,1,0:T(8,128)S(1)}, f32[3,32,8]{2,1,0:T(8,128)S(1)}, u32[]{:S(2)}, u32[]{:S(2)}) collective-permute-start(f32[3,32,8]{2,1,0:T(8,128)S(1)} %shard_map.95), channel_id=1, source_target_pairs={{0,1},{1,0},{2,3},{3,2},{4,5},{5,4},{6,7},{7,6},{8,9},{9,8},{10,11... | collective-permute-start | bytes 9224 | tf_op jit(solution)/shard_map/ppermute | solution.py:20
